TPU v7x, 256 devices: a whole 4x4x8 slice. The times are simulated.
256 devices in a mesh: section: 16 (over x, y), coal: 16 (over z, core).
Axes of the slice: x: 4, y: 4, z: 8, core: 2. Of those that a mesh axis runs over, the one named last changes fastest.
Arguments:
- base_rows: bfloat16 [4, 4608], replicated, may hold values from -6 to 6
- group_out: bfloat16 [10, 4, 4608], replicated, may hold values from -3 to 3
- pre_gain: float32 [16, 4608], P('section'), may hold values from 0.5 to 1.5
- w_query: bfloat16 [16, 4608, 256], P('section'), may hold values from -0.09375 to 0.09375
- w_key: bfloat16 [16, 4608, 128], P('section'), may hold values from -0.09375 to 0.09375
- w_value: bfloat16 [16, 4608, 128], P('section'), may hold values from -0.09375 to 0.09375
- w_out: bfloat16 [16, 256, 4608], P('section'), may hold values from -0.375 to 0.375
- post_gain: float32 [16, 4608], P('section'), may hold values from 0.5 to 1.5
- key_cache: bfloat16 [16, 2048, 128], P('section'), may hold values from -6 to 6
- value_cache: bfloat16 [16, 2048, 128], P('section'), may hold values from -6 to 6
- final_gain: float32 [4608], replicated, may hold values from 0.5 to 1.5
- answer_rows: bfloat16 [4096, 4608], P('section'), may hold values from -0.25 to 0.25
Outputs:
- interactions: float32 [1024, 4, 4096], P('coal', None, 'section')
- shapley: float32 [10, 4, 4096], P(None, None, 'section')
All inputs are finite; a program needn't handle non-finite values.
Results may differ from a plain program's by a relative error of at most 0.0013.
Values sent between devices are 32-bit elements; how exact they have to be, the bound alone decides.
A program may use at most 128 MiB of HBM per device.

v0:
```python
import jax
import jax.numpy as jnp
from jax import lax
from jax.sharding import PartitionSpec as P

MICRO = 16
COALS = 1024


norm_eps = 1e-06
attn_cap = 50.0
logit_cap = 30.0
query_scale = 1.0 / 12.0
highest = lax.Precision.HIGHEST


def shifted(block, axis, distance):
    devices = range(lax.axis_size(axis))
    route = [(i - distance, i) for i in devices if i - distance in devices]
    return lax.ppermute(block, axis, route)


def spread(value, axis, source):
    kept = jnp.where(lax.axis_index(axis) == source, value, 0).astype(value.dtype)
    return lax.psum(kept, axis)


def matmul(left, right):
    return jnp.dot(left, right.astype(jnp.float32), precision=highest)


def rms_scale(values, gain_row):
    return (
        values * lax.rsqrt(jnp.mean(values * values, axis=-1, keepdims=True) + norm_eps) * gain_row
    )


def rotary(values, cosine, sine_table):
    half_dim = values.shape[-1] // 2
    front_half = values[..., :half_dim]
    second = values[..., half_dim:]
    return jnp.concatenate(
        [front_half * cosine - second * sine_table, second * cosine + front_half * sine_table],
        axis=-1,
    )


def rope_tables(prefix_len, seq_len, head_dim):
    half_dim = head_dim // 2
    places = prefix_len + jnp.arange(seq_len, dtype=jnp.float32)
    inverse = 10000.0 ** (-2.0 * jnp.arange(half_dim, dtype=jnp.float32) / head_dim)
    angles = places[:, None] * inverse[None, :]
    return (jnp.cos(angles), jnp.sin(angles))


def attend(
    hidden,
    pre_gain_row,
    w_query,
    w_key,
    w_value,
    w_out,
    post_gain_row,
    keys_old,
    values_old,
    seq_len,
):
    total_rows = hidden.shape[0]
    head_dim = keys_old.shape[1]
    q_heads = w_query.shape[1] // head_dim
    groups_in = total_rows // seq_len
    normed = rms_scale(hidden, pre_gain_row)
    queries = jnp.dot(normed, w_query, precision=highest).reshape(
        groups_in, seq_len, q_heads, head_dim
    )
    key_new = jnp.dot(normed, w_key, precision=highest).reshape(groups_in, seq_len, head_dim)
    value_new = jnp.dot(normed, w_value, precision=highest).reshape(groups_in, seq_len, head_dim)
    cosine, sine_table = rope_tables(keys_old.shape[0], seq_len, head_dim)
    queries = rotary(queries, cosine[:, None, :], sine_table[:, None, :])
    key_new = rotary(key_new, cosine, sine_table)
    past_scores = jnp.einsum("cshd,pd->cshp", queries, keys_old, precision=highest) * query_scale
    recent = jnp.einsum("cshd,ctd->csht", queries, key_new, precision=highest) * query_scale
    causal = jnp.arange(seq_len)[:, None] >= jnp.arange(seq_len)[None, :]
    past_exp = jnp.exp(attn_cap * jnp.tanh(past_scores / attn_cap))
    recent_exp = jnp.where(
        causal[None, :, None, :], jnp.exp(attn_cap * jnp.tanh(recent / attn_cap)), 0.0
    )
    totals = jnp.sum(past_exp, axis=-1, keepdims=True) + jnp.sum(recent_exp, axis=-1, keepdims=True)
    past_weights = past_exp / totals
    recent_weights = recent_exp / totals
    attended = jnp.einsum("cshp,pd->cshd", past_weights, values_old, precision=highest)
    attended = attended + jnp.einsum("csht,ctd->cshd", recent_weights, value_new, precision=highest)
    attended = attended.reshape(total_rows, q_heads * head_dim)
    projected = jnp.dot(attended, w_out, precision=highest)
    return hidden + rms_scale(projected, post_gain_row)


def readout_local(hidden, final_gain, answer_wide):
    normed = rms_scale(hidden, final_gain)
    logits = jnp.einsum("nd,kd->nk", normed, answer_wide, precision=highest)
    capped = logit_cap * jnp.tanh(logits / logit_cap)
    return (capped, jnp.sum(jnp.exp(capped), axis=-1))


def moebius(coeffs, bit_count):
    total_rows = coeffs.shape[0]
    for bit_idx in range(bit_count):
        stride = 1 << bit_idx
        blocks = coeffs.reshape(total_rows // (2 * stride), 2, stride, -1)
        coeffs = jnp.concatenate([blocks[:, :1], blocks[:, 1:] - blocks[:, :1]], axis=1).reshape(
            total_rows, -1
        )
    return coeffs


def shapley_weights(first_id, id_count, groups):
    id_list = first_id + jnp.arange(id_count, dtype=jnp.int32)
    member = (id_list[:, None] >> jnp.arange(groups, dtype=jnp.int32)[None, :] & 1).astype(
        jnp.float32
    )
    set_sizes = jnp.maximum(jnp.sum(member, axis=1, keepdims=True), 1.0)
    return member / set_sizes


def per_device(
    base_rows,
    group_out,
    pre_gain,
    w_query,
    w_key,
    w_value,
    w_out,
    post_gain,
    key_cache,
    value_cache,
    final_gain,
    answer_rows,
):
    sections = lax.axis_size("section")
    my_section = lax.axis_index("section")
    coal_count = lax.axis_size("coal")
    my_block = lax.axis_index("coal")
    coal_local = COALS // coal_count
    seq_len, model_width = base_rows.shape
    groups = group_out.shape[0]
    per_batch = coal_local // MICRO
    batch_rows = per_batch * seq_len
    cand_local = answer_rows.shape[0]
    id_list = my_block * coal_local + jnp.arange(coal_local, dtype=jnp.int32)
    member = (id_list[:, None] >> jnp.arange(groups, dtype=jnp.int32)[None, :] & 1).astype(
        jnp.float32
    )
    mixture = matmul(member, group_out.reshape(groups, seq_len * model_width))
    mixture = mixture + base_rows.reshape(1, seq_len * model_width).astype(jnp.float32)
    starts = mixture.reshape(MICRO, batch_rows, model_width)
    query_wide = w_query[0].astype(jnp.float32)
    key_wide = w_key[0].astype(jnp.float32)
    value_wide = w_value[0].astype(jnp.float32)
    out_wide = w_out[0].astype(jnp.float32)
    keys_old = key_cache[0].astype(jnp.float32)
    values_old = value_cache[0].astype(jnp.float32)
    answer_wide = answer_rows.astype(jnp.float32)

    def run_section(hidden):
        return attend(
            hidden,
            pre_gain[0],
            query_wide,
            key_wide,
            value_wide,
            out_wide,
            post_gain[0],
            keys_old,
            values_old,
            seq_len,
        )

    def advance(tick_idx, incoming):
        batch_idx = tick_idx - my_section
        active = (batch_idx >= 0) & (batch_idx < MICRO)
        fresh_rows = lax.dynamic_index_in_dim(
            starts, jnp.clip(batch_idx, 0, MICRO - 1), 0, keepdims=False
        )
        current = jnp.where(my_section == 0, fresh_rows, incoming)
        result = lax.cond(active, run_section, lambda unchanged: unchanged, current)
        passed = shifted(result, "section", 1)
        return (result, passed)

    empty_rows = jnp.zeros((batch_rows, model_width), jnp.float32)
    last_tick = MICRO + sections - 1

    def plain_tick(tick_idx, state_pair):
        incoming, finished = state_pair
        result, passed = advance(tick_idx, incoming)
        slot_idx = jnp.clip(tick_idx - (sections - 1), 0, MICRO - 1)
        is_done = tick_idx >= sections - 1
        previous = lax.dynamic_index_in_dim(finished, slot_idx, 0, keepdims=False)
        finished = lax.dynamic_update_index_in_dim(
            finished, jnp.where(is_done, result, previous), slot_idx, 0
        )
        return (passed, finished)

    finished = jnp.zeros((MICRO, batch_rows, model_width), jnp.float32)
    incoming, finished = lax.fori_loop(0, last_tick, plain_tick, (empty_rows, finished))
    arrived = spread(finished, "section", sections - 1)
    capped, local_sums = readout_local(
        arrived.reshape(coal_local * seq_len, model_width), final_gain, answer_wide
    )
    totals = lax.psum(local_sums, "section")
    log_probs = (capped - jnp.log(totals)[:, None]).reshape(coal_local, seq_len * cand_local)
    local_bits = coal_local.bit_length() - 1
    remote_bits = coal_count.bit_length() - 1
    coeffs = moebius(log_probs, local_bits)
    for bit_idx in range(remote_bits):
        partner = shifted(coeffs, "coal", 1 << bit_idx)
        has_bit = (my_block >> bit_idx & 1).astype(jnp.float32)
        coeffs = coeffs - has_bit * partner
    weights = shapley_weights(my_block * coal_local, coal_local, groups)
    partial_terms = jnp.einsum("cg,cn->gn", weights, coeffs, precision=highest)
    shapley = lax.psum(partial_terms, "coal")
    return (
        coeffs.reshape(coal_local, seq_len, cand_local),
        shapley.reshape(groups, seq_len, cand_local),
    )


def solution(mesh):
    placed = (
        P(),
        P(),
        P("section", None),
        P("section", None, None),
        P("section", None, None),
        P("section", None, None),
        P("section", None, None),
        P("section", None),
        P("section", None, None),
        P("section", None, None),
        P(),
        P("section", None),
    )
    return jax.shard_map(
        per_device,
        mesh=mesh,
        in_specs=placed,
        out_specs=(P("coal", None, "section"), P(None, None, "section")),
        check_vma=False,
    )
```

profile of v0, /device:TPU:11, one launch (start us, length us, event | category | flops | bytes accessed | tf_op | source)
XLA Modules:
  0.0 1226.8 jit_solution(10546751678034508981)
XLA Ops:
  34.8 797.0 %while.17 = (s32[]{:T(128)}, f32[16,4608]{1,0:T(8,128)S(1)}, f32[16,16,4608]{2,1,0:T(8,128)}, s32[]{:T(128)}, pred[]{:T(512)}, /*index=5*/f32[16,16,4608]{2,1,0:...) while((s32[]{:T(128)}, f32[16,4608]{1,0:T(8,128)S(1)}, ...), condition=%wide.region_7.8_spmd, body=%wide.region_0.7_spmd.sunk | while | flops 882598912 | bytes 42001920 | solution.py:204
  61.5 6.2 collective-permute-done
  82.7 86.2 %collective-permute-done = f32[16,4608]{1,0:T(8,128)S(1)} collective-permute-done((f32[16,4608]{1,0:T(8,128)S(1)}, f32[16,4608]{1,0:T(8,128)S(1)}, u32[]{:S(2)}, u32[]{:S(2)}) %collective-permute-start) | collective-permute-done | bytes 294944 | tf_op jit(solution)/shard_map/while/body/eval_jaxpr/ppermute | solution.py:20
  169.9 19.4 %conditional.2 = (f32[16,4608]{1,0:T(8,128)S(1)}) conditional(s32[]{:T(128)} %convert_element_type.111, f32[16,4608]{1,0:T(8,128)S(1)} %bitcast_select_fusion.3, (f32[16,4608]{1,0:T(8,128)S(1)}, f32[1,4608]{1,0:T(1,128)S(1)}, f32[4608,256]{1,0:T(8,128)}, f32[2048,128]{1,0:T(8,128)}, f32[4608,128]{1,0:T(8,128)}, /*index=5*/f32[2048,128]{1,0:T(8,128)}, ...), branch_computations={%region_1.1_spmd, %region_2.6_spmd} | conditional | flops 882451456 | bytes 38462572 | solution.py:185
  199.8 19.4 %conditional.2 = (f32[16,4608]{1,0:T(8,128)S(1)}) conditional(s32[]{:T(128)} %convert_element_type.111, f32[16,4608]{1,0:T(8,128)S(1)} %bitcast_select_fusion.3, (f32[16,4608]{1,0:T(8,128)S(1)}, f32[1,4608]{1,0:T(1,128)S(1)}, f32[4608,256]{1,0:T(8,128)}, f32[2048,128]{1,0:T(8,128)}, f32[4608,128]{1,0:T(8,128)}, /*index=5*/f32[2048,128]{1,0:T(8,128)}, ...), branch_computations={%region_1.1_spmd, %region_2.6_spmd} | conditional | flops 882451456 | bytes 38462572 | solution.py:185
  229.8 19.4 %conditional.2 = (f32[16,4608]{1,0:T(8,128)S(1)}) conditional(s32[]{:T(128)} %convert_element_type.111, f32[16,4608]{1,0:T(8,128)S(1)} %bitcast_select_fusion.3, (f32[16,4608]{1,0:T(8,128)S(1)}, f32[1,4608]{1,0:T(1,128)S(1)}, f32[4608,256]{1,0:T(8,128)}, f32[2048,128]{1,0:T(8,128)}, f32[4608,128]{1,0:T(8,128)}, /*index=5*/f32[2048,128]{1,0:T(8,128)}, ...), branch_computations={%region_1.1_spmd, %region_2.6_spmd} | conditional | flops 882451456 | bytes 38462572 | solution.py:185
  259.7 19.4 %conditional.2 = (f32[16,4608]{1,0:T(8,128)S(1)}) conditional(s32[]{:T(128)} %convert_element_type.111, f32[16,4608]{1,0:T(8,128)S(1)} %bitcast_select_fusion.3, (f32[16,4608]{1,0:T(8,128)S(1)}, f32[1,4608]{1,0:T(1,128)S(1)}, f32[4608,256]{1,0:T(8,128)}, f32[2048,128]{1,0:T(8,128)}, f32[4608,128]{1,0:T(8,128)}, /*index=5*/f32[2048,128]{1,0:T(8,128)}, ...), branch_computations={%region_1.1_spmd, %region_2.6_spmd} | conditional | flops 882451456 | bytes 38462572 | solution.py:185
  289.6 19.4 %conditional.2 = (f32[16,4608]{1,0:T(8,128)S(1)}) conditional(s32[]{:T(128)} %convert_element_type.111, f32[16,4608]{1,0:T(8,128)S(1)} %bitcast_select_fusion.3, (f32[16,4608]{1,0:T(8,128)S(1)}, f32[1,4608]{1,0:T(1,128)S(1)}, f32[4608,256]{1,0:T(8,128)}, f32[2048,128]{1,0:T(8,128)}, f32[4608,128]{1,0:T(8,128)}, /*index=5*/f32[2048,128]{1,0:T(8,128)}, ...), branch_computations={%region_1.1_spmd, %region_2.6_spmd} | conditional | flops 882451456 | bytes 38462572 | solution.py:185
  319.6 19.4 %conditional.2 = (f32[16,4608]{1,0:T(8,128)S(1)}) conditional(s32[]{:T(128)} %convert_element_type.111, f32[16,4608]{1,0:T(8,128)S(1)} %bitcast_select_fusion.3, (f32[16,4608]{1,0:T(8,128)S(1)}, f32[1,4608]{1,0:T(1,128)S(1)}, f32[4608,256]{1,0:T(8,128)}, f32[2048,128]{1,0:T(8,128)}, f32[4608,128]{1,0:T(8,128)}, /*index=5*/f32[2048,128]{1,0:T(8,128)}, ...), branch_computations={%region_1.1_spmd, %region_2.6_spmd} | conditional | flops 882451456 | bytes 38462572 | solution.py:185
  349.5 19.4 %conditional.2 = (f32[16,4608]{1,0:T(8,128)S(1)}) conditional(s32[]{:T(128)} %convert_element_type.111, f32[16,4608]{1,0:T(8,128)S(1)} %bitcast_select_fusion.3, (f32[16,4608]{1,0:T(8,128)S(1)}, f32[1,4608]{1,0:T(1,128)S(1)}, f32[4608,256]{1,0:T(8,128)}, f32[2048,128]{1,0:T(8,128)}, f32[4608,128]{1,0:T(8,128)}, /*index=5*/f32[2048,128]{1,0:T(8,128)}, ...), branch_computations={%region_1.1_spmd, %region_2.6_spmd} | conditional | flops 882451456 | bytes 38462572 | solution.py:185
  379.4 19.4 %conditional.2 = (f32[16,4608]{1,0:T(8,128)S(1)}) conditional(s32[]{:T(128)} %convert_element_type.111, f32[16,4608]{1,0:T(8,128)S(1)} %bitcast_select_fusion.3, (f32[16,4608]{1,0:T(8,128)S(1)}, f32[1,4608]{1,0:T(1,128)S(1)}, f32[4608,256]{1,0:T(8,128)}, f32[2048,128]{1,0:T(8,128)}, f32[4608,128]{1,0:T(8,128)}, /*index=5*/f32[2048,128]{1,0:T(8,128)}, ...), branch_computations={%region_1.1_spmd, %region_2.6_spmd} | conditional | flops 882451456 | bytes 38462572 | solution.py:185
  409.4 19.4 %conditional.2 = (f32[16,4608]{1,0:T(8,128)S(1)}) conditional(s32[]{:T(128)} %convert_element_type.111, f32[16,4608]{1,0:T(8,128)S(1)} %bitcast_select_fusion.3, (f32[16,4608]{1,0:T(8,128)S(1)}, f32[1,4608]{1,0:T(1,128)S(1)}, f32[4608,256]{1,0:T(8,128)}, f32[2048,128]{1,0:T(8,128)}, f32[4608,128]{1,0:T(8,128)}, /*index=5*/f32[2048,128]{1,0:T(8,128)}, ...), branch_computations={%region_1.1_spmd, %region_2.6_spmd} | conditional | flops 882451456 | bytes 38462572 | solution.py:185
  439.3 19.4 %conditional.2 = (f32[16,4608]{1,0:T(8,128)S(1)}) conditional(s32[]{:T(128)} %convert_element_type.111, f32[16,4608]{1,0:T(8,128)S(1)} %bitcast_select_fusion.3, (f32[16,4608]{1,0:T(8,128)S(1)}, f32[1,4608]{1,0:T(1,128)S(1)}, f32[4608,256]{1,0:T(8,128)}, f32[2048,128]{1,0:T(8,128)}, f32[4608,128]{1,0:T(8,128)}, /*index=5*/f32[2048,128]{1,0:T(8,128)}, ...), branch_computations={%region_1.1_spmd, %region_2.6_spmd} | conditional | flops 882451456 | bytes 38462572 | solution.py:185
  469.2 19.4 %conditional.2 = (f32[16,4608]{1,0:T(8,128)S(1)}) conditional(s32[]{:T(128)} %convert_element_type.111, f32[16,4608]{1,0:T(8,128)S(1)} %bitcast_select_fusion.3, (f32[16,4608]{1,0:T(8,128)S(1)}, f32[1,4608]{1,0:T(1,128)S(1)}, f32[4608,256]{1,0:T(8,128)}, f32[2048,128]{1,0:T(8,128)}, f32[4608,128]{1,0:T(8,128)}, /*index=5*/f32[2048,128]{1,0:T(8,128)}, ...), branch_computations={%region_1.1_spmd, %region_2.6_spmd} | conditional | flops 882451456 | bytes 38462572 | solution.py:185
  499.2 19.4 %conditional.2 = (f32[16,4608]{1,0:T(8,128)S(1)}) conditional(s32[]{:T(128)} %convert_element_type.111, f32[16,4608]{1,0:T(8,128)S(1)} %bitcast_select_fusion.3, (f32[16,4608]{1,0:T(8,128)S(1)}, f32[1,4608]{1,0:T(1,128)S(1)}, f32[4608,256]{1,0:T(8,128)}, f32[2048,128]{1,0:T(8,128)}, f32[4608,128]{1,0:T(8,128)}, /*index=5*/f32[2048,128]{1,0:T(8,128)}, ...), branch_computations={%region_1.1_spmd, %region_2.6_spmd} | conditional | flops 882451456 | bytes 38462572 | solution.py:185
  522.2 5.9 collective-permute-done
  529.1 19.4 %conditional.2 = (f32[16,4608]{1,0:T(8,128)S(1)}) conditional(s32[]{:T(128)} %convert_element_type.111, f32[16,4608]{1,0:T(8,128)S(1)} %bitcast_select_fusion.3, (f32[16,4608]{1,0:T(8,128)S(1)}, f32[1,4608]{1,0:T(1,128)S(1)}, f32[4608,256]{1,0:T(8,128)}, f32[2048,128]{1,0:T(8,128)}, f32[4608,128]{1,0:T(8,128)}, /*index=5*/f32[2048,128]{1,0:T(8,128)}, ...), branch_computations={%region_1.1_spmd, %region_2.6_spmd} | conditional | flops 882451456 | bytes 38462572 | solution.py:185
  559.0 19.4 %conditional.2 = (f32[16,4608]{1,0:T(8,128)S(1)}) conditional(s32[]{:T(128)} %convert_element_type.111, f32[16,4608]{1,0:T(8,128)S(1)} %bitcast_select_fusion.3, (f32[16,4608]{1,0:T(8,128)S(1)}, f32[1,4608]{1,0:T(1,128)S(1)}, f32[4608,256]{1,0:T(8,128)}, f32[2048,128]{1,0:T(8,128)}, f32[4608,128]{1,0:T(8,128)}, /*index=5*/f32[2048,128]{1,0:T(8,128)}, ...), branch_computations={%region_1.1_spmd, %region_2.6_spmd} | conditional | flops 882451456 | bytes 38462572 | solution.py:185
  589.0 19.4 %conditional.2 = (f32[16,4608]{1,0:T(8,128)S(1)}) conditional(s32[]{:T(128)} %convert_element_type.111, f32[16,4608]{1,0:T(8,128)S(1)} %bitcast_select_fusion.3, (f32[16,4608]{1,0:T(8,128)S(1)}, f32[1,4608]{1,0:T(1,128)S(1)}, f32[4608,256]{1,0:T(8,128)}, f32[2048,128]{1,0:T(8,128)}, f32[4608,128]{1,0:T(8,128)}, /*index=5*/f32[2048,128]{1,0:T(8,128)}, ...), branch_computations={%region_1.1_spmd, %region_2.6_spmd} | conditional | flops 882451456 | bytes 38462572 | solution.py:185
  618.9 19.4 %conditional.2 = (f32[16,4608]{1,0:T(8,128)S(1)}) conditional(s32[]{:T(128)} %convert_element_type.111, f32[16,4608]{1,0:T(8,128)S(1)} %bitcast_select_fusion.3, (f32[16,4608]{1,0:T(8,128)S(1)}, f32[1,4608]{1,0:T(1,128)S(1)}, f32[4608,256]{1,0:T(8,128)}, f32[2048,128]{1,0:T(8,128)}, f32[4608,128]{1,0:T(8,128)}, /*index=5*/f32[2048,128]{1,0:T(8,128)}, ...), branch_computations={%region_1.1_spmd, %region_2.6_spmd} | conditional | flops 882451456 | bytes 38462572 | solution.py:185
  646.7 21.3 %collective-permute-start = (f32[16,4608]{1,0:T(8,128)S(1)}, f32[16,4608]{1,0:T(8,128)S(1)}, u32[]{:S(2)}, u32[]{:S(2)}) collective-permute-start(f32[16,4608]{1,0:T(8,128)S(1)} %get-tuple-element.557), channel_id=1, source_target_pairs={{0,16},{16,32},{32,48},{48,64},{64,80},{80,96},{96,112},{112,128},... | collective-permute-start | bytes 884744 | tf_op jit(solution)/shard_map/while/body/eval_jaxpr/ppermute | solution.py:20
  684.8 19.1 %collective-permute-start = (f32[16,4608]{1,0:T(8,128)S(1)}, f32[16,4608]{1,0:T(8,128)S(1)}, u32[]{:S(2)}, u32[]{:S(2)}) collective-permute-start(f32[16,4608]{1,0:T(8,128)S(1)} %get-tuple-element.557), channel_id=1, source_target_pairs={{0,16},{16,32},{32,48},{48,64},{64,80},{80,96},{96,112},{112,128},... | collective-permute-start | bytes 884744 | tf_op jit(solution)/shard_map/while/body/eval_jaxpr/ppermute | solution.py:20
  722.5 21.1 %collective-permute-start = (f32[16,4608]{1,0:T(8,128)S(1)}, f32[16,4608]{1,0:T(8,128)S(1)}, u32[]{:S(2)}, u32[]{:S(2)}) collective-permute-start(f32[16,4608]{1,0:T(8,128)S(1)} %get-tuple-element.557), channel_id=1, source_target_pairs={{0,16},{16,32},{32,48},{48,64},{64,80},{80,96},{96,112},{112,128},... | collective-permute-start | bytes 884744 | tf_op jit(solution)/shard_map/while/body/eval_jaxpr/ppermute | solution.py:20
  760.4 13.7 %collective-permute-start = (f32[16,4608]{1,0:T(8,128)S(1)}, f32[16,4608]{1,0:T(8,128)S(1)}, u32[]{:S(2)}, u32[]{:S(2)}) collective-permute-start(f32[16,4608]{1,0:T(8,128)S(1)} %get-tuple-element.557), channel_id=1, source_target_pairs={{0,16},{16,32},{32,48},{48,64},{64,80},{80,96},{96,112},{112,128},... | collective-permute-start | bytes 884744 | tf_op jit(solution)/shard_map/while/body/eval_jaxpr/ppermute | solution.py:20
  780.4 6.5 collective-permute-start
  794.3 17.3 %collective-permute-start = (f32[16,4608]{1,0:T(8,128)S(1)}, f32[16,4608]{1,0:T(8,128)S(1)}, u32[]{:S(2)}, u32[]{:S(2)}) collective-permute-start(f32[16,4608]{1,0:T(8,128)S(1)} %get-tuple-element.557), channel_id=1, source_target_pairs={{0,16},{16,32},{32,48},{48,64},{64,80},{80,96},{96,112},{112,128},... | collective-permute-start | bytes 884744 | tf_op jit(solution)/shard_map/while/body/eval_jaxpr/ppermute | solution.py:20
  819.0 6.6 collective-permute-start
  834.3 249.0 %all-reduce.2.cloned.1.call-done = f32[16,16,4608]{2,1,0:T(8,128)} async-done(((f32[16,16,4608]{2,1,0:T(8,128)}), f32[16,16,4608]{2,1,0:T(8,128)}) %all-reduce.2.cloned.1.call-update) | async-done | bytes 4718608 | tf_op jit(solution)/shard_map/psum | solution.py:25
  1091.7 25.3 %psum.22 = f32[256]{0:T(256)S(1)} all-reduce(f32[256]{0:T(256)S(1)} %get-tuple-element.409), channel_id=1, replica_groups=mesh['section'=16,'coal'=16] {'section'}, use_global_device_ids=true, to_apply=%region_11.12 | all-reduce | flops 256 | bytes 2048 | tf_op jit(solution)/shard_map/psum | solution.py:209
  1118.7 10.8 collective-permute-start.1
  1140.3 6.8 collective-permute-start.3
  1161.5 58.5 %psum.23 = f32[10,4,256]{2,1,0:T(4,128)} all-reduce(f32[10,4,256]{2,1,0:T(4,128)S(1)} %reshape.239), channel_id=1, replica_groups=mesh['section'=16,'coal'=16] {'coal'}, use_global_device_ids=true, to_apply=%region_13.14 | all-reduce | flops 10240 | bytes 81920 | tf_op jit(solution)/shard_map/psum | solution.py:220
  (643 shorter events, 655.3 us)
Async XLA Ops:
  7.2 1076.2 %all-reduce.2.cloned.1.call-start = ((), (), s32[]{:S(2)}) async-start(), calls=%async_computation | async-start | bytes 9437184 | tf_op jit(solution)/shard_map/psum | solution.py:25
  35.9 9.8 collective-permute-start
  46.6 10.0 collective-permute-start
  57.6 10.0 collective-permute-start
  68.7 9.3 collective-permute-start
  79.0 89.9 %collective-permute-start = (f32[16,4608]{1,0:T(8,128)S(1)}, f32[16,4608]{1,0:T(8,128)S(1)}, u32[]{:S(2)}, u32[]{:S(2)}) collective-permute-start(f32[16,4608]{1,0:T(8,128)S(1)} %get-tuple-element.557), channel_id=1, source_target_pairs={{0,16},{16,32},{32,48},{48,64},{64,80},{80,96},{96,112},{112,128},... | collective-permute-start | bytes 884744 | tf_op jit(solution)/shard_map/while/body/eval_jaxpr/ppermute | solution.py:20
  189.3 9.6 collective-permute-start
  219.2 9.6 collective-permute-start
  249.1 9.6 collective-permute-start
  279.1 9.6 collective-permute-start
  309.0 9.6 collective-permute-start
  338.9 9.6 collective-permute-start
  368.8 9.6 collective-permute-start
  398.8 9.6 collective-permute-start
  428.7 9.6 collective-permute-start
  458.6 9.6 collective-permute-start
  488.6 9.6 collective-permute-start
  518.5 9.6 collective-permute-start
  548.4 9.6 collective-permute-start
  578.4 9.6 collective-permute-start
  608.3 9.6 collective-permute-start
  646.7 25.3 %collective-permute-start = (f32[16,4608]{1,0:T(8,128)S(1)}, f32[16,4608]{1,0:T(8,128)S(1)}, u32[]{:S(2)}, u32[]{:S(2)}) collective-permute-start(f32[16,4608]{1,0:T(8,128)S(1)} %get-tuple-element.557), channel_id=1, source_target_pairs={{0,16},{16,32},{32,48},{48,64},{64,80},{80,96},{96,112},{112,128},... | collective-permute-start | bytes 884744 | tf_op jit(solution)/shard_map/while/body/eval_jaxpr/ppermute | solution.py:20
  673.0 10.8 collective-permute-start
  684.8 25.8 %collective-permute-start = (f32[16,4608]{1,0:T(8,128)S(1)}, f32[16,4608]{1,0:T(8,128)S(1)}, u32[]{:S(2)}, u32[]{:S(2)}) collective-permute-start(f32[16,4608]{1,0:T(8,128)S(1)} %get-tuple-element.557), channel_id=1, source_target_pairs={{0,16},{16,32},{32,48},{48,64},{64,80},{80,96},{96,112},{112,128},... | collective-permute-start | bytes 884744 | tf_op jit(solution)/shard_map/while/body/eval_jaxpr/ppermute | solution.py:20
  711.6 9.9 collective-permute-start
  722.5 26.9 %collective-permute-start = (f32[16,4608]{1,0:T(8,128)S(1)}, f32[16,4608]{1,0:T(8,128)S(1)}, u32[]{:S(2)}, u32[]{:S(2)}) collective-permute-start(f32[16,4608]{1,0:T(8,128)S(1)} %get-tuple-element.557), channel_id=1, source_target_pairs={{0,16},{16,32},{32,48},{48,64},{64,80},{80,96},{96,112},{112,128},... | collective-permute-start | bytes 884744 | tf_op jit(solution)/shard_map/while/body/eval_jaxpr/ppermute | solution.py:20
  760.4 19.0 %collective-permute-start = (f32[16,4608]{1,0:T(8,128)S(1)}, f32[16,4608]{1,0:T(8,128)S(1)}, u32[]{:S(2)}, u32[]{:S(2)}) collective-permute-start(f32[16,4608]{1,0:T(8,128)S(1)} %get-tuple-element.557), channel_id=1, source_target_pairs={{0,16},{16,32},{32,48},{48,64},{64,80},{80,96},{96,112},{112,128},... | collective-permute-start | bytes 884744 | tf_op jit(solution)/shard_map/while/body/eval_jaxpr/ppermute | solution.py:20
  780.4 12.9 %collective-permute-start = (f32[16,4608]{1,0:T(8,128)S(1)}, f32[16,4608]{1,0:T(8,128)S(1)}, u32[]{:S(2)}, u32[]{:S(2)}) collective-permute-start(f32[16,4608]{1,0:T(8,128)S(1)} %get-tuple-element.557), channel_id=1, source_target_pairs={{0,16},{16,32},{32,48},{48,64},{64,80},{80,96},{96,112},{112,128},... | collective-permute-start | bytes 884744 | tf_op jit(solution)/shard_map/while/body/eval_jaxpr/ppermute | solution.py:20
  794.3 23.6 %collective-permute-start = (f32[16,4608]{1,0:T(8,128)S(1)}, f32[16,4608]{1,0:T(8,128)S(1)}, u32[]{:S(2)}, u32[]{:S(2)}) collective-permute-start(f32[16,4608]{1,0:T(8,128)S(1)} %get-tuple-element.557), channel_id=1, source_target_pairs={{0,16},{16,32},{32,48},{48,64},{64,80},{80,96},{96,112},{112,128},... | collective-permute-start | bytes 884744 | tf_op jit(solution)/shard_map/while/body/eval_jaxpr/ppermute | solution.py:20
  819.0 12.8 %collective-permute-start = (f32[16,4608]{1,0:T(8,128)S(1)}, f32[16,4608]{1,0:T(8,128)S(1)}, u32[]{:S(2)}, u32[]{:S(2)}) collective-permute-start(f32[16,4608]{1,0:T(8,128)S(1)} %get-tuple-element.557), channel_id=1, source_target_pairs={{0,16},{16,32},{32,48},{48,64},{64,80},{80,96},{96,112},{112,128},... | collective-permute-start | bytes 884744 | tf_op jit(solution)/shard_map/while/body/eval_jaxpr/ppermute | solution.py:20
  1118.7 14.1 %collective-permute-start.1 = (f32[64,1024]{1,0:T(8,128)S(1)}, f32[64,1024]{1,0:T(8,128)S(1)}, u32[]{:S(2)}, u32[]{:S(2)}) collective-permute-start(f32[64,1024]{1,0:T(8,128)S(1)} %bitcast.92), channel_id=1, source_target_pairs={{0,1},{1,2},{2,3},{3,4},{4,5},{5,6},{6,7},{7,8},{8,9},{9,10},{10,1... | collective-permute-start | bytes 786440 | tf_op jit(solution)/shard_map/ppermute | solution.py:20
  1140.3 11.6 collective-permute-start.3
  (27 other events, 1580.4 us)
Sparse Core Ops, SparseCore 0:
  834.5 248.8 all-reduce.1
where the time goes:
time: 1240 us; the launch traced here: 1230 us
  waiting for transfers between devices  505 us (41%)
  matrix products  303 us (24%)
  starting transfers between devices  187 us (15%)
  other arithmetic  86.8 us (7%)
  blocking collectives  83.8 us (7%)
  local copies, waits for them, and re-layouts  44.3 us (4%)
  between operations  14.3 us (1%)
    ppermute x35, waiting for transfers between devices, shifted(): return lax.ppermute(block, axis, route)  256 us
    psum x1, waiting for transfers between devices, spread(): return lax.psum(kept, axis)  249 us
    ppermute x35, starting transfers between devices, shifted(): return lax.ppermute(block, axis, route)  187 us
    dot_general x16, matrix products, attend(): jnp.dot(normed, w_query, precision=highest)  70.4 us
    psum x1, blocking collectives, per_device(): shapley = lax.psum(partial_terms, 'coal')  58.5 us
    dot_general x16, matrix products, attend(): jnp.dot(normed, w_key, precision=highest)  47.4 us
    dot_general x16, matrix products, attend(): jnp.dot(normed, w_value, precision=highest)  47.3 us
    dot_general x16, matrix products, attend(): jnp.einsum('cshd,pd->cshp', queries, keys_old, precision=highest)  43.8 us
  transfers between devices with their start and end apart: 36, of which 36 were waited for; matrix products, arithmetic and copies ran while one was open for 4% of the time, Pallas kernels for 0%

commit v1 on v0

v1 whole, which is shorter than its diff:
```python
import functools

import jax
import jax.numpy as jnp
import numpy as np
from jax import lax
from jax.experimental import pallas as pl
from jax.experimental.pallas import tpu as pltpu
from jax.sharding import PartitionSpec as P

f32, bf16 = jnp.float32, jnp.bfloat16
MESH = pl.DeviceIdType.MESH

D = 4608
HEAD = 128
PREFIX = 2048
GROUPS = 10
SECTIONS = 16
COALS = 16
R = 8
M = 32
CANDS = 256
EPS = 1e-6
LAST = SECTIONS - 1
MAX_LAG = 2 * LAST + 2 * 5 + 2


def rope_rows():
    half = HEAD // 2
    places = PREFIX + np.arange(R) % 4
    inverse = 10000.0 ** (-2.0 * np.arange(half) / HEAD)
    angles = places[:, None] * inverse[None, :]
    cosine, sine = np.cos(angles), np.sin(angles)
    return (
        np.concatenate([cosine, cosine], axis=1).astype(np.float32),
        np.concatenate([-sine, sine], axis=1).astype(np.float32),
    )


def split2(x):
    high = x.astype(bf16).astype(f32)
    return jnp.concatenate([high, x - high], axis=0).astype(bf16)


def fold(y):
    half = y.shape[0] // 2
    return y[:half] + y[half:]


def dot(left, right):
    return jnp.dot(left, right, preferred_element_type=f32)


def block(x, w_ref, wo_ref, kt_ref, v_ref, pre, post, cosine, sine):
    rows = x.shape[0]
    inv = lax.rsqrt(jnp.mean(x * x, axis=-1, keepdims=True) + EPS)
    y = fold(dot(split2(x * pre), w_ref[...])) * inv

    def rotated(z):
        return z * cosine + pltpu.roll(z, HEAD // 2, 1) * sine

    q = jnp.concatenate([rotated(y[:, :128]), rotated(y[:, 128:256])], axis=0)
    q = q * (1.0 / 600.0)
    k = rotated(y[:, 256:384])
    v = y[:, 384:512]
    p = jnp.exp(50.0 * jnp.tanh(fold(dot(split2(q), kt_ref[...]))))
    mixed = fold(dot(split2(p), v_ref[...]))
    total = jnp.sum(p, axis=-1, keepdims=True)
    place = lax.broadcasted_iota(jnp.int32, (2 * rows, 1), 0) % 4
    for back in range(4):
        k_back = pltpu.roll(k, back, 0) if back else k
        v_back = pltpu.roll(v, back, 0) if back else v
        score = jnp.sum(
            q * jnp.concatenate([k_back, k_back], axis=0), axis=-1, keepdims=True
        )
        weight = jnp.where(place >= back, jnp.exp(50.0 * jnp.tanh(score)), 0.0)
        total = total + weight
        mixed = mixed + weight * jnp.concatenate([v_back, v_back], axis=0)
    attended = mixed / total
    attended = jnp.concatenate([attended[:rows], attended[rows:]], axis=1)
    proj = fold(dot(split2(attended), wo_ref[...]))
    scale = lax.rsqrt(jnp.mean(proj * proj, axis=-1, keepdims=True) + EPS)
    return x + proj * scale * post


def shapley_weights(first_id):
    shape = (16 * 8, 256)
    row = lax.broadcasted_iota(jnp.int32, shape, 0)
    column = lax.broadcasted_iota(jnp.int32, shape, 1)
    group = row // 8
    ident = first_id + column // 4
    size = jnp.zeros(shape, jnp.int32)
    for g in range(GROUPS):
        size = size + ((ident >> g) & 1)
    has = (ident >> group) & 1
    others = size - has
    weight = jnp.zeros(shape, f32)
    fact = [1.0]
    for n in range(1, GROUPS + 1):
        fact.append(fact[-1] * n)
    for n in range(GROUPS):
        value = fact[n] * fact[GROUPS - 1 - n] / fact[GROUPS]
        weight = jnp.where(others == n, value, weight)
    weight = jnp.where(has == 1, weight, -weight)
    return jnp.where((row % 4 == column % 4) & (group < GROUPS), weight, 0.0)


def kernel(
    base_ref,
    group_ref,
    pre_ref,
    post_ref,
    fin_gain_ref,
    cos_ref,
    sin_ref,
    wq_hbm,
    wk_hbm,
    wv_hbm,
    wo_hbm,
    key_hbm,
    val_hbm,
    ans_hbm,
    out_ref,
    shap_ref,
    w,
    wo,
    key,
    kt,
    val,
    ans,
    groups,
    rows,
    fin,
    capped,
    sums,
    send1,
    recv1,
    send2,
    recv2,
    init_sem,
    chain_recv,
    chain_send,
    fin_recv,
    fin_send,
    small_sem,
):
    l = lax.axis_index("section")
    c = lax.axis_index("coal")
    y = lax.rem(l, 4)
    x = l // 4

    loads = [
        (wq_hbm, w.at[:, pl.ds(0, 256)]),
        (wk_hbm, w.at[:, pl.ds(256, 128)]),
        (wv_hbm, w.at[:, pl.ds(384, 128)]),
        (wo_hbm, wo),
        (key_hbm, key),
        (val_hbm, val),
        (ans_hbm, ans),
    ]
    loads = [
        pltpu.make_async_copy(a, b, init_sem.at[i]) for i, (a, b) in enumerate(loads)
    ]
    for load in loads:
        load.start()

    barrier = pltpu.get_barrier_semaphore()

    def greet(k, carry):
        pl.semaphore_signal(
            barrier, inc=1, device_id=(lax.rem(l + k, SECTIONS), c), device_id_type=MESH
        )
        pl.semaphore_signal(
            barrier, inc=1, device_id=(l, lax.rem(c + k, COALS)), device_id_type=MESH
        )
        return carry

    lax.fori_loop(1, 16, greet, 0)
    pl.semaphore_wait(barrier, 30)

    for load in loads:
        load.wait()
    kt[...] = key[...].T

    @pl.when(l == 0)
    def _():
        g = group_ref[...].astype(f32)
        groups[...] = jnp.concatenate([g, g], axis=1)

    def chain_copy(b):
        return pltpu.make_async_remote_copy(
            src_ref=rows.at[b],
            dst_ref=rows.at[b],
            send_sem=chain_send,
            recv_sem=chain_recv.at[b],
            device_id=(lax.rem(l + 1, SECTIONS), c),
            device_id_type=MESH,
        )

    def fin_copy(b, child, sem):
        return pltpu.make_async_remote_copy(
            src_ref=fin.at[b],
            dst_ref=fin.at[b],
            send_sem=fin_send.at[sem],
            recv_sem=fin_recv.at[b],
            device_id=(child, c),
            device_id_type=MESH,
        )

    def spread(b):
        @pl.when(y > 0)
        def _():
            fin_copy(b, l - 1, 0).start()

        @pl.when((l == 15) | (l == 11))
        def _():
            fin_copy(b, l - 4, 1).start()

        @pl.when(l == 15)
        def _():
            fin_copy(b, 3, 2).start()

    def work(b):
        @pl.when(l == 0)
        def _():
            ident = c * 64 + 2 * b + lax.broadcasted_iota(jnp.int32, (R, 1), 0) // 4
            b32 = base_ref[...].astype(f32)
            acc = jnp.concatenate([b32, b32], axis=0)
            for g in range(GROUPS):
                acc = acc + ((ident >> g) & 1).astype(f32) * groups[g]
            rows[b] = acc

        @pl.when(l > 0)
        def _():
            chain_copy(b).wait_recv()

        new = block(
            rows[b], w, wo, kt, val, pre_ref[...], post_ref[...], cos_ref[...], sin_ref[...]
        )

        @pl.when(l < LAST)
        def _():
            rows[b] = new
            chain_copy(b).start()

        @pl.when(l == LAST)
        def _():
            inv = lax.rsqrt(jnp.mean(new * new, axis=-1, keepdims=True) + EPS)
            fin[b] = new * inv * fin_gain_ref[...]
            spread(b)

    away = jnp.where(x == 3, 0, jnp.where(x == 1, 2, 1)) + 3 - y
    lag = 2 * (LAST - l) + 2 * away + 2

    def tick(t, carry):
        @pl.when(t < M)
        def _():
            work(t)

        b = t - lag

        @pl.when((l < LAST) & (b >= 0) & (b < M))
        def _():
            fin_copy(b, l, 0).wait_recv()
            spread(b)

        return carry

    lax.fori_loop(0, M + MAX_LAG, tick, 0)

    def whole(ref, sem):
        return pltpu.make_async_remote_copy(
            src_ref=ref,
            dst_ref=ref,
            send_sem=sem,
            recv_sem=sem,
            device_id=(l, c),
            device_id_type=MESH,
        )

    flat = 128

    def read(i, carry):
        part = fin[pl.ds(i * (flat // R), flat // R)].reshape(flat, D)
        logits = fold(
            lax.dot_general(
                split2(part),
                ans[...],
                (((1,), (1,)), ((), ())),
                preferred_element_type=f32,
            )
        )
        capped[pl.ds(i * flat, flat)] = 30.0 * jnp.tanh(logits * (1.0 / 30.0))
        return carry

    lax.fori_loop(0, 256 // flat, read, 0)

    eye = lax.broadcasted_iota(jnp.int32, (128, 128), 0) == lax.broadcasted_iota(
        jnp.int32, (128, 128), 1
    )
    own = []
    for h in range(2):
        part = jnp.sum(
            jnp.exp(capped[pl.ds(128 * h, 128)]), axis=-1, keepdims=True
        )
        own.append(jnp.sum(jnp.where(eye, part, 0.0), axis=0, keepdims=True))
    sums[l] = jnp.concatenate(own + [jnp.zeros((6, 128), f32)], axis=0)

    def sums_copy(peer):
        return pltpu.make_async_remote_copy(
            src_ref=sums.at[l],
            dst_ref=sums.at[l],
            send_sem=small_sem.at[0],
            recv_sem=small_sem.at[1],
            device_id=(peer, c),
            device_id_type=MESH,
        )

    def send_sums(k, carry):
        sums_copy(lax.rem(l + k, SECTIONS)).start()
        return carry

    lax.fori_loop(1, 16, send_sums, 0)
    all_sums = whole(sums.at[pl.ds(0, 15)], small_sem.at[0])
    all_sums.wait_send()
    whole(sums.at[pl.ds(0, 15)], small_sem.at[1]).wait_recv()
    logs = jnp.log(jnp.sum(sums[...], axis=0))
    for h in range(2):
        column = jnp.sum(
            jnp.where(eye, logs[h : h + 1, :], 0.0), axis=1, keepdims=True
        )
        capped[pl.ds(128 * h, 128)] = capped[pl.ds(128 * h, 128)] - column

    values = capped[...]
    shap = jnp.dot(
        shapley_weights(c * 64),
        values,
        preferred_element_type=f32,
        precision=lax.Precision.HIGHEST,
    )
    coeffs = values.reshape(M, R, CANDS)
    upper = lax.broadcasted_iota(jnp.int32, (M, R, CANDS), 1) >= 4
    lower = jnp.concatenate([coeffs[:, 4:], coeffs[:, :4]], axis=1)
    coeffs = coeffs - jnp.where(upper, lower, 0.0)
    for bit in range(5):
        step = 1 << bit
        pairs = coeffs.reshape(M // (2 * step), 2, step, R, CANDS)
        coeffs = jnp.concatenate(
            [pairs[:, :1], pairs[:, 1:] - pairs[:, :1]], axis=1
        ).reshape(M, R, CANDS)
    send1[:, 0:2] = coeffs.reshape(16, 2, R, CANDS)
    send1[:, 2] = shap.reshape(16, 8, CANDS)
    recv1[c] = send1[c]

    def copy1(peer):
        return pltpu.make_async_remote_copy(
            src_ref=send1.at[peer],
            dst_ref=recv1.at[c],
            send_sem=small_sem.at[2],
            recv_sem=small_sem.at[3],
            device_id=(l, peer),
            device_id_type=MESH,
        )

    def start1(k, carry):
        copy1(lax.rem(c + k, COALS)).start()
        return carry

    lax.fori_loop(1, 16, start1, 0)
    whole(send1.at[pl.ds(0, 15)], small_sem.at[2]).wait_send()
    whole(recv1.at[pl.ds(0, 15)], small_sem.at[3]).wait_recv()

    got = recv1[:, 0:2]
    for bit in range(4):
        step = 1 << bit
        pairs = got.reshape(COALS // (2 * step), 2, step, 2, R, CANDS)
        got = jnp.concatenate(
            [pairs[:, :1], pairs[:, 1:] - pairs[:, :1]], axis=1
        ).reshape(COALS, 2, R, CANDS)
    send2[:, 0:2] = got
    total = jnp.sum(recv1[:, 2], axis=0)
    send2[:, 2] = jnp.broadcast_to(total[None], (COALS, R, CANDS))
    recv2[c] = send2[c]

    def copy2(peer):
        return pltpu.make_async_remote_copy(
            src_ref=send2.at[peer],
            dst_ref=recv2.at[c],
            send_sem=small_sem.at[4],
            recv_sem=small_sem.at[5],
            device_id=(l, peer),
            device_id_type=MESH,
        )

    def start2(k, carry):
        copy2(lax.rem(c + k, COALS)).start()
        return carry

    lax.fori_loop(1, 16, start2, 0)
    whole(send2.at[pl.ds(0, 15)], small_sem.at[4]).wait_send()
    whole(recv2.at[pl.ds(0, 15)], small_sem.at[5]).wait_recv()
    out_ref[...] = recv2[:, 0:2].reshape(M, R, CANDS)
    shap_ref[...] = recv2[0:GROUPS, 2]

    @pl.when(l < LAST)
    def _():
        whole(rows, chain_send).wait_send()

    @pl.when(y > 0)
    def _():
        whole(fin, fin_send.at[0]).wait_send()

    @pl.when((l == 15) | (l == 11))
    def _():
        whole(fin, fin_send.at[1]).wait_send()

    @pl.when(l == 15)
    def _():
        whole(fin, fin_send.at[2]).wait_send()


def per_device(
    base_rows,
    group_out,
    pre_gain,
    w_query,
    w_key,
    w_value,
    w_out,
    post_gain,
    key_cache,
    value_cache,
    final_gain,
    answer_rows,
):
    cosine, sine = rope_rows()
    vmem = pl.BlockSpec(memory_space=pltpu.VMEM)
    hbm = pl.BlockSpec(memory_space=pl.ANY)
    exchange = pltpu.VMEM((16, 3, R, CANDS), f32)
    coeffs, shapley = pl.pallas_call(
        kernel,
        out_shape=(
            jax.ShapeDtypeStruct((M, R, CANDS), f32),
            jax.ShapeDtypeStruct((GROUPS, 8, CANDS), f32),
        ),
        in_specs=[vmem] * 7 + [hbm] * 7,
        out_specs=(vmem, vmem),
        scratch_shapes=[
            pltpu.VMEM((D, 512), bf16),
            pltpu.VMEM((256, D), bf16),
            pltpu.VMEM((PREFIX, HEAD), bf16),
            pltpu.VMEM((HEAD, PREFIX), bf16),
            pltpu.VMEM((PREFIX, HEAD), bf16),
            pltpu.VMEM((CANDS, D), bf16),
            pltpu.VMEM((GROUPS, R, D), f32),
            pltpu.VMEM((M, R, D), f32),
            pltpu.VMEM((M, R, D), f32),
            pltpu.VMEM((M * R, CANDS), f32),
            pltpu.VMEM((SECTIONS, 8, 128), f32),
            exchange,
            exchange,
            exchange,
            exchange,
            pltpu.SemaphoreType.DMA((7,)),
            pltpu.SemaphoreType.DMA((M,)),
            pltpu.SemaphoreType.DMA,
            pltpu.SemaphoreType.DMA((M,)),
            pltpu.SemaphoreType.DMA((3,)),
            pltpu.SemaphoreType.DMA((6,)),
        ],
        compiler_params=pltpu.CompilerParams(
            collective_id=0, has_side_effects=True, vmem_limit_bytes=58 << 20
        ),
    )(
        base_rows,
        group_out,
        pre_gain,
        post_gain,
        final_gain.reshape(1, D),
        jnp.asarray(cosine),
        jnp.asarray(sine),
        w_query[0],
        w_key[0],
        w_value[0],
        w_out[0],
        key_cache[0],
        value_cache[0],
        answer_rows,
    )
    return coeffs.reshape(64, 4, CANDS), shapley[:, :4]


def solution(mesh):
    placed = (
        P(),
        P(),
        P("section", None),
        P("section", None, None),
        P("section", None, None),
        P("section", None, None),
        P("section", None, None),
        P("section", None),
        P("section", None, None),
        P("section", None, None),
        P(),
        P("section", None),
    )
    return jax.shard_map(
        per_device,
        mesh=mesh,
        in_specs=placed,
        out_specs=(P("coal", None, "section"), P(None, None, "section")),
        check_vma=False,
    )
```

time: 1240 us -> 275 us (0.22)
  waiting for transfers between devices: 505 us -> 0 us
  matrix products: 303 us -> 0 us
  Pallas kernels: 0 us -> 268 us
  starting transfers between devices: 187 us -> 0 us
  other arithmetic: 86.8 us -> 0 us
  blocking collectives: 83.8 us -> 0 us
  local copies, waits for them, and re-layouts: 44.3 us -> 4.58 us
  between operations: 14.3 us -> 0.64 us
    dot_general x131 -> x0, matrix products: 303 us -> none  [the longest x16 70.4 us: attend(): jnp.dot(normed, w_query, precision=highest)]
    pallas_call x0 -> x1, Pallas kernels: none -> 268 us  [per_device(): pl.pallas_call(kernel, out_shape=(jax.ShapeDtypeStruct((M, R, CANDS), f32...]
    ppermute x35 -> x0, waiting for transfers between devices: 256 us -> none  [shifted(): return lax.ppermute(block, axis, route)]
    psum x1 -> x0, waiting for transfers between devices: 249 us -> none  [spread(): return lax.psum(kept, axis)]
    ppermute x35 -> x0, starting transfers between devices: 187 us -> none  [shifted(): return lax.ppermute(block, axis, route)]
    psum x2 -> x0, blocking collectives: 83.8 us -> none  [the longest x1 58.5 us: per_device(): shapley = lax.psum(partial_terms, 'coal')]
    select_n x32 -> x0, other arithmetic: 33.3 us -> none  [the longest x31 30.8 us: advance(): current = jnp.where(my_section == 0, fresh_rows, incoming)]
    dynamic_slice x31 -> x0, local copies, waits for them, and re-layouts: 30.6 us -> none  [plain_tick(): previous = lax.dynamic_index_in_dim(finished, slot_idx, 0, keepdims=False)]
  transfers between devices with their start and end apart: 36 -> 0, of which waited for: 36 -> 0; matrix products, arithmetic and copies ran while one was open for 4% -> 0% of each run, Pallas kernels for 0% -> 0%
where the time goes in v1:
time: 275 us; the launch traced here: 273 us
  Pallas kernels  268 us (97%)
  local copies, waits for them, and re-layouts  4.58 us (2%)
    pallas_call x1, Pallas kernels, per_device(): pl.pallas_call(kernel, out_shape=(jax.ShapeDtypeStruct((M, R, CANDS), f32...  268 us

profile of v1, /device:TPU:11, one launch (start us, length us, event | category | flops | bytes accessed | tf_op | source)
XLA Modules:
  0.0 272.8 jit_solution(1311896406940528099)
XLA Ops:
  0.6 1.3 reshape.10.fin_gain_ref
  2.0 267.6 %shard_map.149 = (f32[32,8,256]{2,1,0:T(8,128)}, f32[10,8,256]{2,1,0:T(8,128)}) custom-call(bf16[4,4608]{1,0:T(4,128)(2,1)} %base_ref.1, bf16[10,4,4608]{2,1,0:T(4,128)(2,1)} %group_ref.1, f32[1,4608]{1,0:T(1,128)} %pre_ref.1, f32[1,4608]{1,0:T(1,128)} %post_ref.1, f32[1,4608]{1,0:T(1,128)} %reshape.10.fin_gain_ref, f32[8,128]{1,0:T(8,128)} %constant.4.clone.cos_ref, ...), custom_call_target="tpu_custom_call" | custom-call | tf_op jit(solution)/shard_map/pallas_call | solution.py:440
  269.6 1.7 reshape.11
  271.3 1.5 slice.3

commit v2 on v1

v2 whole, which is shorter than its diff:
```python
import functools

import jax
import jax.numpy as jnp
import numpy as np
from jax import lax
from jax.experimental import pallas as pl
from jax.experimental.pallas import tpu as pltpu
from jax.sharding import PartitionSpec as P

f32, bf16 = jnp.float32, jnp.bfloat16
MESH = pl.DeviceIdType.MESH

D = 4608
HEAD = 128
PREFIX = 2048
GROUPS = 10
SECTIONS = 16
COALS = 16
R = 8
M = 32
CANDS = 256
EPS = 1e-6
LAST = SECTIONS - 1
CHUNKS = 4
DEPTH = 3
WIDE = D // CHUNKS
GROUP = 8
N_GROUPS = M // GROUP
G_ROWS = GROUP * R
HOP = 60
MAX_LAG = 40
LATE = 26


def rope_rows():
    half = HEAD // 2
    places = PREFIX + np.arange(R) % 4
    inverse = 10000.0 ** (-2.0 * np.arange(half) / HEAD)
    angles = places[:, None] * inverse[None, :]
    cosine, sine = np.cos(angles), np.sin(angles)
    return (
        np.concatenate([cosine, cosine], axis=1).astype(np.float32),
        np.concatenate([-sine, sine], axis=1).astype(np.float32),
    )


def split2(x):
    high = x.astype(bf16).astype(f32)
    return jnp.concatenate([high, x - high], axis=0).astype(bf16)


def fold(y):
    half = y.shape[0] // 2
    return y[:half] + y[half:]


def dot(left, right):
    return jnp.dot(left, right, preferred_element_type=f32)


def attention(y, kt_ref, v_ref, cosine, sine):
    rows = y.shape[0]

    def rotated(z):
        return z * cosine + pltpu.roll(z, HEAD // 2, 1) * sine

    q = jnp.concatenate([rotated(y[:, :128]), rotated(y[:, 128:256])], axis=0)
    q = q * (1.0 / 600.0)
    k = rotated(y[:, 256:384])
    v = y[:, 384:512]
    p = jnp.exp(50.0 * jnp.tanh(fold(dot(split2(q), kt_ref[...]))))
    mixed = fold(dot(split2(p), v_ref[...]))
    total = jnp.sum(p, axis=-1, keepdims=True)
    place = lax.broadcasted_iota(jnp.int32, (2 * rows, 1), 0) % 4
    for back in range(4):
        k_back = pltpu.roll(k, back, 0) if back else k
        v_back = pltpu.roll(v, back, 0) if back else v
        score = jnp.sum(
            q * jnp.concatenate([k_back, k_back], axis=0), axis=-1, keepdims=True
        )
        weight = jnp.where(place >= back, jnp.exp(50.0 * jnp.tanh(score)), 0.0)
        total = total + weight
        mixed = mixed + weight * jnp.concatenate([v_back, v_back], axis=0)
    attended = mixed / total
    return jnp.concatenate([attended[:rows], attended[rows:]], axis=1)


def shapley_weights(first_id):
    shape = (16 * 8, G_ROWS)
    row = lax.broadcasted_iota(jnp.int32, shape, 0)
    column = lax.broadcasted_iota(jnp.int32, shape, 1)
    group = row // 8
    ident = first_id + column // 4
    size = jnp.zeros(shape, jnp.int32)
    for g in range(GROUPS):
        size = size + ((ident >> g) & 1)
    has = (ident >> group) & 1
    others = size - has
    weight = jnp.zeros(shape, f32)
    fact = [1.0]
    for n in range(1, GROUPS + 1):
        fact.append(fact[-1] * n)
    for n in range(GROUPS):
        value = fact[n] * fact[GROUPS - 1 - n] / fact[GROUPS]
        weight = jnp.where(others == n, value, weight)
    weight = jnp.where(has == 1, weight, -weight)
    return jnp.where((row % 4 == column % 4) & (group < GROUPS), weight, 0.0)


def kernel(
    base_ref,
    group_ref,
    pre_ref,
    post_ref,
    fin_gain_ref,
    cos_ref,
    sin_ref,
    wq_hbm,
    wk_hbm,
    wv_hbm,
    wo_hbm,
    key_hbm,
    val_hbm,
    ans_hbm,
    out_ref,
    shap_ref,
    w,
    wo,
    key,
    kt,
    val,
    ans,
    ans_t,
    groups,
    rows,
    fin,
    capped,
    sums,
    send1,
    recv1,
    send2,
    recv2,
    init_sem,
    chain_recv,
    chain_send,
    fin_recv,
    fin_send,
    tail_send,
    tail_recv,
):
    l = lax.axis_index("section")
    c = lax.axis_index("coal")
    y = lax.rem(l, 4)
    x = l // 4

    loads = [
        (wq_hbm, w.at[:, pl.ds(0, 256)]),
        (wk_hbm, w.at[:, pl.ds(256, 128)]),
        (wv_hbm, w.at[:, pl.ds(384, 128)]),
        (key_hbm, key),
        (val_hbm, val),
        (wo_hbm, wo),
        (ans_hbm, ans),
    ]
    loads = [
        pltpu.make_async_copy(a, b, init_sem.at[i]) for i, (a, b) in enumerate(loads)
    ]
    for load in loads:
        load.start()

    barrier = pltpu.get_barrier_semaphore()

    def greet(k, carry):
        pl.semaphore_signal(
            barrier, inc=1, device_id=(lax.rem(l + k, SECTIONS), c), device_id_type=MESH
        )
        pl.semaphore_signal(
            barrier, inc=1, device_id=(l, lax.rem(c + k, COALS)), device_id_type=MESH
        )
        return carry

    lax.fori_loop(1, 16, greet, 0)

    @pl.when(l == 0)
    def _():
        g = group_ref[...].astype(f32)
        groups[...] = jnp.concatenate([g, g], axis=1)

    for load in loads:
        load.wait()
    kt[...] = key[...].T

    def turn_answers():
        def turn(i, carry):
            at = pl.multiple_of(i * 128, 128)
            ans_t[pl.ds(at, 128), :] = ans[:, pl.ds(at, 128)].T
            return carry

        lax.fori_loop(0, D // 128, turn, 0)

    @pl.when(l > 0)
    def _():
        turn_answers()

    pl.semaphore_wait(barrier, 30)

    def part(j):
        return pl.ds(j * WIDE, WIDE)

    def chain_copy(b, j):
        return pltpu.make_async_remote_copy(
            src_ref=rows.at[b, :, part(j)],
            dst_ref=rows.at[b, :, part(j)],
            send_sem=chain_send.at[lax.rem(b, DEPTH)],
            recv_sem=chain_recv.at[b, j],
            device_id=(lax.rem(l + 1, SECTIONS), c),
            device_id_type=MESH,
        )

    def fin_copy(b, child, sem):
        return pltpu.make_async_remote_copy(
            src_ref=fin.at[b],
            dst_ref=fin.at[b],
            send_sem=fin_send.at[sem],
            recv_sem=fin_recv.at[b],
            device_id=(child, c),
            device_id_type=MESH,
        )

    def spread(b):
        @pl.when((l == 15) | (l == 11))
        def _():
            fin_copy(b, l - 4, 1).start()

        @pl.when(l == 15)
        def _():
            fin_copy(b, 3, 2).start()

        @pl.when((y > 1) | ((y == 1) & (b < LATE)))
        def _():
            fin_copy(b, l - 1, 0).start()

        @pl.when((y == 3) & (b >= LATE))
        def _():
            fin_copy(b, l - 3, 3).start()

    def whole(ref, sem):
        return pltpu.make_async_remote_copy(
            src_ref=ref,
            dst_ref=ref,
            send_sem=sem,
            recv_sem=sem,
            device_id=(l, c),
            device_id_type=MESH,
        )

    def work(b):
        @pl.when(l == 0)
        def _():
            ident = c * 64 + 2 * b + lax.broadcasted_iota(jnp.int32, (R, 1), 0) // 4
            b32 = base_ref[...].astype(f32)
            acc = jnp.concatenate([b32, b32], axis=0)
            for g in range(GROUPS):
                acc = acc + ((ident >> g) & 1).astype(f32) * groups[g]
            rows[b] = acc

        square = jnp.zeros((R, 1), f32)
        mixed = jnp.zeros((2 * R, 512), f32)
        for j in range(CHUNKS):

            @pl.when(l > 0)
            def _():
                chain_copy(b, j).wait_recv()

            piece = rows[b, :, part(j)]
            square = square + jnp.sum(piece * piece, axis=-1, keepdims=True)
            mixed = mixed + dot(split2(piece * pre_ref[:, part(j)]), w[part(j), :])
        inv = lax.rsqrt(square * (1.0 / D) + EPS)
        attended = attention(fold(mixed) * inv, kt, val, cos_ref[...], sin_ref[...])
        proj = fold(dot(split2(attended), wo[...]))
        scale = lax.rsqrt(jnp.mean(proj * proj, axis=-1, keepdims=True) + EPS)

        @pl.when((l < LAST) & (b >= DEPTH))
        def _():
            whole(rows.at[b - DEPTH], chain_send.at[lax.rem(b, DEPTH)]).wait_send()

        @pl.when(l < LAST)
        def _():
            for j in range(CHUNKS):
                rows[b, :, part(j)] = (
                    rows[b, :, part(j)]
                    + proj[:, j * WIDE : (j + 1) * WIDE] * scale * post_ref[:, part(j)]
                )
                chain_copy(b, j).start()

        @pl.when(l == LAST)
        def _():
            new = rows[b] + proj * scale * post_ref[...]
            inv = lax.rsqrt(jnp.mean(new * new, axis=-1, keepdims=True) + EPS)
            fin[b] = new * inv * fin_gain_ref[...]
            spread(b)

    eye = lax.broadcasted_iota(jnp.int32, (G_ROWS, 128), 0) == lax.broadcasted_iota(
        jnp.int32, (G_ROWS, 128), 1
    )

    def read(g):
        block = fin[pl.ds(g * GROUP, GROUP)].reshape(G_ROWS, D)
        logits = fold(dot(split2(block), ans_t[...]))
        values = 30.0 * jnp.tanh(logits * (1.0 / 30.0))
        capped[g] = values
        column = jnp.sum(jnp.exp(values), axis=-1, keepdims=True)
        line = jnp.sum(jnp.where(eye, column, 0.0), axis=0, keepdims=True)
        mine = g * SECTIONS + l
        sums[mine] = jnp.broadcast_to(line, (8, 128))

        def send(k, carry):
            pltpu.make_async_remote_copy(
                src_ref=sums.at[mine],
                dst_ref=sums.at[mine],
                send_sem=tail_send.at[0],
                recv_sem=tail_recv.at[0, g],
                device_id=(lax.rem(l + k, SECTIONS), c),
                device_id_type=MESH,
            ).start()
            return carry

        lax.fori_loop(1, 16, send, 0)

    def exchange(src, dst, g, kind):
        def send(k, carry):
            peer = lax.rem(c + k, COALS)
            pltpu.make_async_remote_copy(
                src_ref=src.at[g * COALS + peer],
                dst_ref=dst.at[g * COALS + c],
                send_sem=tail_send.at[kind],
                recv_sem=tail_recv.at[kind, g],
                device_id=(l, peer),
                device_id_type=MESH,
            ).start()
            return carry

        lax.fori_loop(1, 16, send, 0)
        dst[g * COALS + c] = src[g * COALS + c]

    def scatter(g):
        whole(sums.at[pl.ds(0, 15)], tail_recv.at[0, g]).wait_recv()
        logs = jnp.log(jnp.sum(sums[pl.ds(g * SECTIONS, SECTIONS)], axis=0)[0:1])
        column = jnp.sum(jnp.where(eye, logs, 0.0), axis=1, keepdims=True)
        values = capped[g] - column
        shap = jnp.dot(
            shapley_weights(c * 64 + g * (2 * GROUP)),
            values,
            preferred_element_type=f32,
            precision=lax.Precision.HIGHEST,
        ).reshape(16, 8, CANDS)
        low = lax.broadcasted_iota(jnp.int32, (16, 8, 128), 1) < 4
        shap = jnp.where(low, shap[:, :, :128], shap[:, :, 128:])
        values = values.reshape(GROUP, R, CANDS)
        for i in range(GROUP):
            for h in range(2):
                send1[g * COALS + 2 * i + h, 0] = values[i, :, 128 * h : 128 * h + 128]
        send1[pl.ds(g * COALS, COALS), 1] = shap
        exchange(send1, recv1, g, 1)

    def gather(g):
        whole(recv1.at[pl.ds(0, 15)], tail_recv.at[1, g]).wait_recv()
        slots = pl.ds(g * COALS, COALS)
        got = recv1[slots, 0]
        for bit in range(4):
            step = 1 << bit
            pairs = got.reshape(COALS // (2 * step), 2, step, 8, 128)
            got = jnp.concatenate(
                [pairs[:, :1], pairs[:, 1:] - pairs[:, :1]], axis=1
            ).reshape(COALS, 8, 128)
        total = jnp.sum(recv1[slots, 1], axis=0)
        send2[slots, 0] = got
        send2[slots, 1] = jnp.broadcast_to(total[None], (COALS, 8, 128))
        exchange(send2, recv2, g, 2)

    away = jnp.where(x == 3, 0, jnp.where(x == 1, 2, 1)) + 3 - y
    lag = (HOP * (LAST - l) + 10 + 45 * away + 32) // 33
    lag = jnp.where(l == LAST, 0, jnp.where(l == 0, MAX_LAG, lag))

    def tick(t, carry):
        @pl.when(t < M)
        def _():
            work(t)

        @pl.when((l == 0) & (t == M))
        def _():
            turn_answers()

        b = t - lag

        @pl.when((l < LAST) & (b >= 0) & (b < M))
        def _():
            fin_copy(b, l, 0).wait_recv()
            spread(b)

        @pl.when((b >= 0) & (b < M) & (lax.rem(b, GROUP) == GROUP - 1))
        def _():
            read(b // GROUP)

        @pl.when((b >= 18) & (lax.rem(b, GROUP) == 2) & (b <= M + 10))
        def _():
            scatter(b // GROUP - 2)

        @pl.when((b >= 20) & (lax.rem(b, GROUP) == 4) & (b <= M + 12))
        def _():
            gather(b // GROUP - 2)

        return carry

    lax.fori_loop(0, M + MAX_LAG + 13, tick, 0)

    for g in range(N_GROUPS):
        whole(recv2.at[pl.ds(0, 15)], tail_recv.at[2, g]).wait_recv()
    coeffs = recv2[:, 0].reshape(M, 2, 8, 128)
    coeffs = jnp.concatenate([coeffs[:, 0], coeffs[:, 1]], axis=-1)
    upper = lax.broadcasted_iota(jnp.int32, (M, R, CANDS), 1) >= 4
    lower = jnp.concatenate([coeffs[:, 4:], coeffs[:, :4]], axis=1)
    coeffs = coeffs - jnp.where(upper, lower, 0.0)
    for bit in range(5):
        step = 1 << bit
        pairs = coeffs.reshape(M // (2 * step), 2, step, R, CANDS)
        coeffs = jnp.concatenate(
            [pairs[:, :1], pairs[:, 1:] - pairs[:, :1]], axis=1
        ).reshape(M, R, CANDS)
    out_ref[...] = coeffs
    shap_ref[...] = jnp.sum(
        recv2[:, 1].reshape(N_GROUPS, COALS, 8, 128), axis=0
    )[:GROUPS]

    for kind, ref in enumerate([sums, send1, send2]):
        whole(ref.at[pl.ds(0, 15 * N_GROUPS)], tail_send.at[kind]).wait_send()

    @pl.when(l < LAST)
    def _():
        for b in range(M - DEPTH, M):
            whole(rows.at[b], chain_send.at[b % DEPTH]).wait_send()

    @pl.when(y > 1)
    def _():
        whole(fin, fin_send.at[0]).wait_send()

    @pl.when(y == 1)
    def _():
        whole(fin.at[pl.ds(0, LATE)], fin_send.at[0]).wait_send()

    @pl.when(y == 3)
    def _():
        whole(fin.at[pl.ds(LATE, M - LATE)], fin_send.at[3]).wait_send()

    @pl.when((l == 15) | (l == 11))
    def _():
        whole(fin, fin_send.at[1]).wait_send()

    @pl.when(l == 15)
    def _():
        whole(fin, fin_send.at[2]).wait_send()


def per_device(
    base_rows,
    group_out,
    pre_gain,
    w_query,
    w_key,
    w_value,
    w_out,
    post_gain,
    key_cache,
    value_cache,
    final_gain,
    answer_rows,
):
    cosine, sine = rope_rows()
    vmem = pl.BlockSpec(memory_space=pltpu.VMEM)
    hbm = pl.BlockSpec(memory_space=pl.ANY)
    exchange = pltpu.VMEM((N_GROUPS * COALS, 2, 8, 128), f32)
    coeffs, shapley = pl.pallas_call(
        kernel,
        out_shape=(
            jax.ShapeDtypeStruct((M, R, CANDS), f32),
            jax.ShapeDtypeStruct((GROUPS, 8, 128), f32),
        ),
        in_specs=[vmem] * 7 + [hbm] * 7,
        out_specs=(vmem, vmem),
        scratch_shapes=[
            pltpu.VMEM((D, 512), bf16),
            pltpu.VMEM((256, D), bf16),
            pltpu.VMEM((PREFIX, HEAD), bf16),
            pltpu.VMEM((HEAD, PREFIX), bf16),
            pltpu.VMEM((PREFIX, HEAD), bf16),
            pltpu.VMEM((CANDS, D), bf16),
            pltpu.VMEM((D, CANDS), bf16),
            pltpu.VMEM((GROUPS, R, D), f32),
            pltpu.VMEM((M, R, D), f32),
            pltpu.VMEM((M, R, D), f32),
            pltpu.VMEM((N_GROUPS, G_ROWS, CANDS), f32),
            pltpu.VMEM((N_GROUPS * SECTIONS, 8, 128), f32),
            exchange,
            exchange,
            exchange,
            exchange,
            pltpu.SemaphoreType.DMA((7,)),
            pltpu.SemaphoreType.DMA((M, CHUNKS)),
            pltpu.SemaphoreType.DMA((DEPTH,)),
            pltpu.SemaphoreType.DMA((M,)),
            pltpu.SemaphoreType.DMA((4,)),
            pltpu.SemaphoreType.DMA((3,)),
            pltpu.SemaphoreType.DMA((3, N_GROUPS)),
        ],
        compiler_params=pltpu.CompilerParams(
            collective_id=0, has_side_effects=True, vmem_limit_bytes=58 << 20
        ),
    )(
        base_rows,
        group_out,
        pre_gain,
        post_gain,
        final_gain.reshape(1, D),
        jnp.asarray(cosine),
        jnp.asarray(sine),
        w_query[0],
        w_key[0],
        w_value[0],
        w_out[0],
        key_cache[0],
        value_cache[0],
        answer_rows,
    )
    shapley = shapley.reshape(GROUPS, 2, 4, 128).transpose(0, 2, 1, 3)
    return coeffs.reshape(64, 4, CANDS), shapley.reshape(GROUPS, 4, CANDS)


def solution(mesh):
    placed = (
        P(),
        P(),
        P("section", None),
        P("section", None, None),
        P("section", None, None),
        P("section", None, None),
        P("section", None, None),
        P("section", None),
        P("section", None, None),
        P("section", None, None),
        P(),
        P("section", None),
    )
    return jax.shard_map(
        per_device,
        mesh=mesh,
        in_specs=placed,
        out_specs=(P("coal", None, "section"), P(None, None, "section")),
        check_vma=False,
    )
```

time: 275 us -> 262 us (0.953)
  Pallas kernels: 268 us -> 256 us
    pallas_call x1, Pallas kernels: 268 us -> 256 us  [per_device(): pl.pallas_call(kernel, out_shape=(jax.ShapeDtypeStruct((M, R, CANDS), f32...]
where the time goes in v2:
time: 262 us; the launch traced here: 261 us
  Pallas kernels  256 us (98%)
  local copies, waits for them, and re-layouts  4.47 us (2%)
    pallas_call x1, Pallas kernels, per_device(): pl.pallas_call(kernel, out_shape=(jax.ShapeDtypeStruct((M, R, CANDS), f32...  256 us

profile of v2, /device:TPU:11, one launch (start us, length us, event | category | flops | bytes accessed | tf_op | source)
XLA Modules:
  0.0 261.4 jit_solution(11440151768918796708)
XLA Ops:
  0.6 1.3 reshape.16.fin_gain_ref
  2.0 256.3 %shard_map.149 = (f32[32,8,256]{2,1,0:T(8,128)}, f32[10,8,128]{2,1,0:T(8,128)}) custom-call(bf16[4,4608]{1,0:T(4,128)(2,1)} %base_ref.1, bf16[10,4,4608]{2,1,0:T(4,128)(2,1)} %group_ref.1, f32[1,4608]{1,0:T(1,128)} %pre_ref.1, f32[1,4608]{1,0:T(1,128)} %post_ref.1, f32[1,4608]{1,0:T(1,128)} %reshape.16.fin_gain_ref, f32[8,128]{1,0:T(8,128)} %constant.4.clone.cos_ref, ...), custom_call_target="tpu_custom_call" | custom-call | tf_op jit(solution)/shard_map/pallas_call | solution.py:483
  258.3 1.7 reshape.17
  260.0 1.4 copy.18

commit v3 on v2

--- a/solution.py
+++ b/solution.py
@@ -25,11 +25,17 @@
 CHUNKS = 4
 DEPTH = 3
 WIDE = D // CHUNKS
-GROUP = 8
+GROUP = 16
+HALF = GROUP // 2
 N_GROUPS = M // GROUP
 G_ROWS = GROUP * R
+END = 2
+E_ROWS = END * R
 HOP = 60
 MAX_LAG = 40
+FAR_FIRST = (8, 7, 9, 6, 10, 5, 11, 4, 12, 3, 13, 2, 14, 1, 15)
+FIN_CHUNKS = 4
+FIN_WIDE = D // FIN_CHUNKS
 LATE = 26
 
 
@@ -86,12 +92,11 @@
     return jnp.concatenate([attended[:rows], attended[rows:]], axis=1)
 
 
-def shapley_weights(first_id):
-    shape = (16 * 8, G_ROWS)
+def shapley_weights(shape, ident_of):
     row = lax.broadcasted_iota(jnp.int32, shape, 0)
     column = lax.broadcasted_iota(jnp.int32, shape, 1)
     group = row // 8
-    ident = first_id + column // 4
+    ident = ident_of(column)
     size = jnp.zeros(shape, jnp.int32)
     for g in range(GROUPS):
         size = size + ((ident >> g) & 1)
@@ -141,6 +146,8 @@
     recv1,
     send2,
     recv2,
+    ends,
+    lines,
     init_sem,
     chain_recv,
     chain_send,
@@ -171,27 +178,39 @@
 
     barrier = pltpu.get_barrier_semaphore()
 
-    def greet(k, carry):
-        pl.semaphore_signal(
-            barrier, inc=1, device_id=(lax.rem(l + k, SECTIONS), c), device_id_type=MESH
-        )
-        pl.semaphore_signal(
-            barrier, inc=1, device_id=(l, lax.rem(c + k, COALS)), device_id_type=MESH
-        )
-        return carry
-
-    lax.fori_loop(1, 16, greet, 0)
+    def greet(device):
+        pl.semaphore_signal(barrier, inc=1, device_id=device, device_id_type=MESH)
+
+    def greet_coal():
+        for k in range(1, COALS):
+            greet((l, lax.rem(c + k, COALS)))
+
+    @pl.when(l == 0)
+    def _():
+        greet_coal()
+
+    for k in range(SECTIONS):
+
+        @pl.when(l != k)
+        def _():
+            greet((k, c))
+
+    @pl.when(l != 0)
+    def _():
+        greet_coal()
 
     @pl.when(l == 0)
     def _():
         g = group_ref[...].astype(f32)
         groups[...] = jnp.concatenate([g, g], axis=1)
 
-    for load in loads:
+    for load in loads[:-1]:
         load.wait()
     kt[...] = key[...].T
 
     def turn_answers():
+        loads[-1].wait()
+
         def turn(i, carry):
             at = pl.multiple_of(i * 128, 128)
             ans_t[pl.ds(at, 128), :] = ans[:, pl.ds(at, 128)].T
@@ -218,32 +237,33 @@
             device_id_type=MESH,
         )
 
-    def fin_copy(b, child, sem):
+    def fin_copy(b, f, child, sem):
+        piece = fin.at[b, :, pl.ds(f * FIN_WIDE, FIN_WIDE)]
         return pltpu.make_async_remote_copy(
-            src_ref=fin.at[b],
-            dst_ref=fin.at[b],
+            src_ref=piece,
+            dst_ref=piece,
             send_sem=fin_send.at[sem],
-            recv_sem=fin_recv.at[b],
+            recv_sem=fin_recv.at[b, f],
             device_id=(child, c),
             device_id_type=MESH,
         )
 
-    def spread(b):
+    def spread(b, f):
         @pl.when((l == 15) | (l == 11))
         def _():
-            fin_copy(b, l - 4, 1).start()
+            fin_copy(b, f, l - 4, 1).start()
 
         @pl.when(l == 15)
         def _():
-            fin_copy(b, 3, 2).start()
+            fin_copy(b, f, 3, 2).start()
 
         @pl.when((y > 1) | ((y == 1) & (b < LATE)))
         def _():
-            fin_copy(b, l - 1, 0).start()
+            fin_copy(b, f, l - 1, 0).start()
 
         @pl.when((y == 3) & (b >= LATE))
         def _():
-            fin_copy(b, l - 3, 3).start()
+            fin_copy(b, f, l - 3, 3).start()
 
     def whole(ref, sem):
         return pltpu.make_async_remote_copy(
@@ -298,38 +318,119 @@
         def _():
             new = rows[b] + proj * scale * post_ref[...]
             inv = lax.rsqrt(jnp.mean(new * new, axis=-1, keepdims=True) + EPS)
-            fin[b] = new * inv * fin_gain_ref[...]
-            spread(b)
-
-    eye = lax.broadcasted_iota(jnp.int32, (G_ROWS, 128), 0) == lax.broadcasted_iota(
-        jnp.int32, (G_ROWS, 128), 1
-    )
-
-    def read(g):
-        block = fin[pl.ds(g * GROUP, GROUP)].reshape(G_ROWS, D)
+            fin[b] = new * inv * fin_gain_ref[...].reshape(1, D)
+            for f in range(FIN_CHUNKS):
+                spread(b, f)
+
+    def eye(shape):
+        return lax.broadcasted_iota(jnp.int32, shape, len(shape) - 2) == (
+            lax.broadcasted_iota(jnp.int32, shape, len(shape) - 1)
+        )
+
+    def score(first, count):
+        block = fin[pl.ds(first, count)].reshape(count * R, D)
         logits = fold(dot(split2(block), ans_t[...]))
-        values = 30.0 * jnp.tanh(logits * (1.0 / 30.0))
-        capped[g] = values
+        return 30.0 * jnp.tanh(logits * (1.0 / 30.0))
+
+    def line_of(values, lane):
+        n = values.shape[0]
         column = jnp.sum(jnp.exp(values), axis=-1, keepdims=True)
-        line = jnp.sum(jnp.where(eye, column, 0.0), axis=0, keepdims=True)
+        here = lax.broadcasted_iota(jnp.int32, (n, 128), 0) + lane
+        here = here == lax.broadcasted_iota(jnp.int32, (n, 128), 1)
+        line = jnp.sum(jnp.where(here, column, 0.0), axis=0, keepdims=True)
+        return jnp.broadcast_to(line, (8, 128))
+
+    def read(first, count, g, lane):
+        values = score(first, count)
+        capped[g, pl.ds(lane, count * R)] = values
         mine = g * SECTIONS + l
-        sums[mine] = jnp.broadcast_to(line, (8, 128))
-
-        def send(k, carry):
+        line = line_of(values, lane)
+        sums[mine] = line if lane == 0 else sums[mine] + line
+
+    def send_sums(slot):
+        mine = slot * SECTIONS + l
+        for k in FAR_FIRST:
             pltpu.make_async_remote_copy(
                 src_ref=sums.at[mine],
                 dst_ref=sums.at[mine],
                 send_sem=tail_send.at[0],
-                recv_sem=tail_recv.at[0, g],
+                recv_sem=tail_recv.at[0, slot],
                 device_id=(lax.rem(l + k, SECTIONS), c),
                 device_id_type=MESH,
             ).start()
-            return carry
-
-        lax.fori_loop(1, 16, send, 0)
+
+    def read_end():
+        values = score(M - END, END)
+        ends[c] = values
+        sums[N_GROUPS * SECTIONS + l] = line_of(values, 0)
+        send_sums(N_GROUPS)
+        for k in FAR_FIRST:
+            end_copy(lax.rem(c + k, COALS)).start()
+
+    def end_copy(peer):
+        return pltpu.make_async_remote_copy(
+            src_ref=ends.at[c],
+            dst_ref=ends.at[c],
+            send_sem=tail_send.at[3],
+            recv_sem=tail_recv.at[1, N_GROUPS],
+            device_id=(l, peer),
+            device_id_type=MESH,
+        )
+
+    def logs_of(slot):
+        whole(sums.at[pl.ds(0, 15)], tail_recv.at[0, slot]).wait_recv()
+        return jnp.log(jnp.sum(sums[pl.ds(slot * SECTIONS, SECTIONS)], axis=0))
+
+    def end_logs():
+        lines[c] = logs_of(N_GROUPS)
+        for k in FAR_FIRST:
+            pltpu.make_async_remote_copy(
+                src_ref=lines.at[c],
+                dst_ref=lines.at[c],
+                send_sem=tail_send.at[4],
+                recv_sem=tail_recv.at[2, N_GROUPS],
+                device_id=(l, lax.rem(c + k, COALS)),
+                device_id_type=MESH,
+            ).start()
+
+    def end_result():
+        def ident(column):
+            return column // E_ROWS * 64 + (64 - 2 * END) + lax.rem(column, E_ROWS) // 4
+
+        weights = shapley_weights((16 * 8, COALS * E_ROWS), ident)
+        signs = []
+        for other in range(COALS):
+            sign = 1
+            for bit in range(4):
+                has = (c >> bit) & 1
+                sign = sign * (has if (other >> bit) & 1 else 1 - 2 * has)
+            signs.append(sign.astype(f32))
+        whole(ends.at[pl.ds(0, 15)], tail_recv.at[1, N_GROUPS]).wait_recv()
+        whole(lines.at[pl.ds(0, 15)], tail_recv.at[2, N_GROUPS]).wait_recv()
+        logs = jnp.sum(
+            jnp.where(eye((COALS, E_ROWS, 128)), lines[:, 0:1, :], 0.0),
+            axis=-1,
+            keepdims=True,
+        )
+        values = ends[...] - logs
+        coeffs = signs[0] * values[0]
+        for other in range(1, COALS):
+            coeffs = coeffs + signs[other] * values[other]
+        shap = jnp.dot(
+            weights,
+            values.reshape(COALS * E_ROWS, CANDS),
+            preferred_element_type=f32,
+            precision=lax.Precision.HIGHEST,
+        )
+        return coeffs.reshape(END, R, CANDS), halves(shap)
+
+    def halves(shap):
+        shap = shap.reshape(16, 8, CANDS)
+        low = lax.broadcasted_iota(jnp.int32, (16, 8, 128), 1) < 4
+        return jnp.where(low, shap[:, :, :128], shap[:, :, 128:])
 
     def exchange(src, dst, g, kind):
-        def send(k, carry):
+        for k in FAR_FIRST:
             peer = lax.rem(c + k, COALS)
             pltpu.make_async_remote_copy(
                 src_ref=src.at[g * COALS + peer],
@@ -339,45 +440,43 @@
                 device_id=(l, peer),
                 device_id_type=MESH,
             ).start()
-            return carry
-
-        lax.fori_loop(1, 16, send, 0)
         dst[g * COALS + c] = src[g * COALS + c]
 
-    def scatter(g):
-        whole(sums.at[pl.ds(0, 15)], tail_recv.at[0, g]).wait_recv()
-        logs = jnp.log(jnp.sum(sums[pl.ds(g * SECTIONS, SECTIONS)], axis=0)[0:1])
-        column = jnp.sum(jnp.where(eye, logs, 0.0), axis=1, keepdims=True)
-        values = capped[g] - column
+    def scatter(g, count):
+        n = count * R
+        column = jnp.sum(
+            jnp.where(eye((n, 128)), logs_of(g)[0:1], 0.0), axis=1, keepdims=True
+        )
+        values = capped[g, pl.ds(0, n)] - column
+        first = c * 64 + g * (2 * GROUP)
         shap = jnp.dot(
-            shapley_weights(c * 64 + g * (2 * GROUP)),
+            shapley_weights((16 * 8, n), lambda column: first + column // 4),
             values,
             preferred_element_type=f32,
             precision=lax.Precision.HIGHEST,
-        ).reshape(16, 8, CANDS)
-        low = lax.broadcasted_iota(jnp.int32, (16, 8, 128), 1) < 4
-        shap = jnp.where(low, shap[:, :, :128], shap[:, :, 128:])
-        values = values.reshape(GROUP, R, CANDS)
-        for i in range(GROUP):
-            for h in range(2):
-                send1[g * COALS + 2 * i + h, 0] = values[i, :, 128 * h : 128 * h + 128]
-        send1[pl.ds(g * COALS, COALS), 1] = shap
-        exchange(send1, recv1, g, 1)
+        )
+        values = values.reshape(count, R, CANDS)
+        for h in range(2):
+            send1[pl.ds(g * COALS, count), h] = values[:, :, 128 * h : 128 * h + 128]
+            if count < GROUP:
+                send1[pl.ds(g * COALS + count, GROUP - count), h] = jnp.zeros(
+                    (GROUP - count, 8, 128), f32
+                )
+        send1[pl.ds(g * COALS, COALS), 2] = halves(shap)
 
     def gather(g):
         whole(recv1.at[pl.ds(0, 15)], tail_recv.at[1, g]).wait_recv()
         slots = pl.ds(g * COALS, COALS)
-        got = recv1[slots, 0]
+        got = recv1[slots, 0:2]
         for bit in range(4):
             step = 1 << bit
-            pairs = got.reshape(COALS // (2 * step), 2, step, 8, 128)
+            pairs = got.reshape(COALS // (2 * step), 2, step, 2, 8, 128)
             got = jnp.concatenate(
                 [pairs[:, :1], pairs[:, 1:] - pairs[:, :1]], axis=1
-            ).reshape(COALS, 8, 128)
-        total = jnp.sum(recv1[slots, 1], axis=0)
-        send2[slots, 0] = got
-        send2[slots, 1] = jnp.broadcast_to(total[None], (COALS, 8, 128))
-        exchange(send2, recv2, g, 2)
+            ).reshape(COALS, 2, 8, 128)
+        total = jnp.sum(recv1[slots, 2], axis=0)
+        send2[slots, 0:2] = got
+        send2[slots, 2] = jnp.broadcast_to(total[None], (COALS, 8, 128))
 
     away = jnp.where(x == 3, 0, jnp.where(x == 1, 2, 1)) + 3 - y
     lag = (HOP * (LAST - l) + 10 + 45 * away + 32) // 33
@@ -396,29 +495,75 @@
 
         @pl.when((l < LAST) & (b >= 0) & (b < M))
         def _():
-            fin_copy(b, l, 0).wait_recv()
-            spread(b)
-
-        @pl.when((b >= 0) & (b < M) & (lax.rem(b, GROUP) == GROUP - 1))
-        def _():
-            read(b // GROUP)
-
-        @pl.when((b >= 18) & (lax.rem(b, GROUP) == 2) & (b <= M + 10))
-        def _():
-            scatter(b // GROUP - 2)
-
-        @pl.when((b >= 20) & (lax.rem(b, GROUP) == 4) & (b <= M + 12))
-        def _():
-            gather(b // GROUP - 2)
+            for f in range(FIN_CHUNKS):
+                fin_copy(b, f, l, 0).wait_recv()
+                spread(b, f)
+
+        @pl.when(b == HALF - 1)
+        def _():
+            read(0, HALF, 0, 0)
+
+        @pl.when(b == GROUP - 1)
+        def _():
+            read(HALF, HALF, 0, HALF * R)
+
+        @pl.when(b == GROUP)
+        def _():
+            send_sums(0)
+
+        @pl.when(b == GROUP + 6)
+        def _():
+            scatter(0, GROUP)
+
+        @pl.when(b == GROUP + HALF - 1)
+        def _():
+            read(GROUP, HALF, 1, 0)
+
+        @pl.when(b == GROUP + HALF)
+        def _():
+            exchange(send1, recv1, 0, 1)
+
+        @pl.when(b == GROUP + HALF + 3)
+        def _():
+            gather(0)
+
+        @pl.when(b == GROUP + HALF + 4)
+        def _():
+            exchange(send2, recv2, 0, 2)
+
+        @pl.when(b == M - END - 1)
+        def _():
+            read(GROUP + HALF, HALF - END, 1, HALF * R)
+            send_sums(1)
+
+        @pl.when(b == M - 1)
+        def _():
+            read_end()
+
+        @pl.when(b == M)
+        def _():
+            scatter(1, GROUP - END)
+            exchange(send1, recv1, 1, 1)
+
+        @pl.when(b == M + 1)
+        def _():
+            end_logs()
+
+        @pl.when(b == M + 2)
+        def _():
+            gather(1)
+            exchange(send2, recv2, 1, 2)
 
         return carry
 
-    lax.fori_loop(0, M + MAX_LAG + 13, tick, 0)
+    lax.fori_loop(0, M + MAX_LAG + 3, tick, 0)
+
+    end_coeffs, end_shap = end_result()
 
     for g in range(N_GROUPS):
         whole(recv2.at[pl.ds(0, 15)], tail_recv.at[2, g]).wait_recv()
-    coeffs = recv2[:, 0].reshape(M, 2, 8, 128)
-    coeffs = jnp.concatenate([coeffs[:, 0], coeffs[:, 1]], axis=-1)
+    coeffs = jnp.concatenate([recv2[:, 0], recv2[:, 1]], axis=-1)
+    coeffs = jnp.concatenate([coeffs[: M - END], end_coeffs], axis=0)
     upper = lax.broadcasted_iota(jnp.int32, (M, R, CANDS), 1) >= 4
     lower = jnp.concatenate([coeffs[:, 4:], coeffs[:, :4]], axis=1)
     coeffs = coeffs - jnp.where(upper, lower, 0.0)
@@ -428,13 +573,22 @@
         coeffs = jnp.concatenate(
             [pairs[:, :1], pairs[:, 1:] - pairs[:, :1]], axis=1
         ).reshape(M, R, CANDS)
-    out_ref[...] = coeffs
-    shap_ref[...] = jnp.sum(
-        recv2[:, 1].reshape(N_GROUPS, COALS, 8, 128), axis=0
-    )[:GROUPS]
-
-    for kind, ref in enumerate([sums, send1, send2]):
-        whole(ref.at[pl.ds(0, 15 * N_GROUPS)], tail_send.at[kind]).wait_send()
+    out_ref[:, 0] = coeffs[:, :4]
+    out_ref[:, 1] = coeffs[:, 4:]
+    shap = jnp.sum(recv2[:, 2].reshape(N_GROUPS, COALS, 8, 128), axis=0)
+    shap = (shap + end_shap)[:GROUPS]
+    shap_ref[:, :, :128] = shap[:, :4]
+    shap_ref[:, :, 128:] = shap[:, 4:]
+
+    waits = [
+        (sums, 15 * (N_GROUPS + 1)),
+        (send1, 15 * N_GROUPS),
+        (send2, 15 * N_GROUPS),
+        (ends, 15),
+        (lines, 15),
+    ]
+    for kind, (ref, count) in enumerate(waits):
+        whole(ref.at[pl.ds(0, count)], tail_send.at[kind]).wait_send()
 
     @pl.when(l < LAST)
     def _():
@@ -479,12 +633,12 @@
     cosine, sine = rope_rows()
     vmem = pl.BlockSpec(memory_space=pltpu.VMEM)
     hbm = pl.BlockSpec(memory_space=pl.ANY)
-    exchange = pltpu.VMEM((N_GROUPS * COALS, 2, 8, 128), f32)
+    exchange = pltpu.VMEM((N_GROUPS * COALS, 3, 8, 128), f32)
     coeffs, shapley = pl.pallas_call(
         kernel,
         out_shape=(
-            jax.ShapeDtypeStruct((M, R, CANDS), f32),
-            jax.ShapeDtypeStruct((GROUPS, 8, 128), f32),
+            jax.ShapeDtypeStruct((M, 2, 4, CANDS), f32),
+            jax.ShapeDtypeStruct((GROUPS, 4, CANDS), f32),
         ),
         in_specs=[vmem] * 7 + [hbm] * 7,
         out_specs=(vmem, vmem),
@@ -500,18 +654,20 @@
             pltpu.VMEM((M, R, D), f32),
             pltpu.VMEM((M, R, D), f32),
             pltpu.VMEM((N_GROUPS, G_ROWS, CANDS), f32),
-            pltpu.VMEM((N_GROUPS * SECTIONS, 8, 128), f32),
+            pltpu.VMEM(((N_GROUPS + 1) * SECTIONS, 8, 128), f32),
             exchange,
             exchange,
             exchange,
             exchange,
+            pltpu.VMEM((COALS, E_ROWS, CANDS), f32),
+            pltpu.VMEM((COALS, 8, 128), f32),
             pltpu.SemaphoreType.DMA((7,)),
             pltpu.SemaphoreType.DMA((M, CHUNKS)),
             pltpu.SemaphoreType.DMA((DEPTH,)),
-            pltpu.SemaphoreType.DMA((M,)),
+            pltpu.SemaphoreType.DMA((M, FIN_CHUNKS)),
             pltpu.SemaphoreType.DMA((4,)),
-            pltpu.SemaphoreType.DMA((3,)),
-            pltpu.SemaphoreType.DMA((3, N_GROUPS)),
+            pltpu.SemaphoreType.DMA((5,)),
+            pltpu.SemaphoreType.DMA((3, N_GROUPS + 1)),
         ],
         compiler_params=pltpu.CompilerParams(
             collective_id=0, has_side_effects=True, vmem_limit_bytes=58 << 20
@@ -521,7 +677,7 @@
         group_out,
         pre_gain,
         post_gain,
-        final_gain.reshape(1, D),
+        final_gain,
         jnp.asarray(cosine),
         jnp.asarray(sine),
         w_query[0],
@@ -532,8 +688,7 @@
         value_cache[0],
         answer_rows,
     )
-    shapley = shapley.reshape(GROUPS, 2, 4, 128).transpose(0, 2, 1, 3)
-    return coeffs.reshape(64, 4, CANDS), shapley.reshape(GROUPS, 4, CANDS)
+    return coeffs.reshape(64, 4, CANDS), shapley
 
 
 def solution(mesh):

time: 262 us -> 251 us (0.958)
  Pallas kernels: 256 us -> 247 us
    pallas_call x1, Pallas kernels: 256 us -> 247 us  [per_device(): pl.pallas_call(kernel, out_shape=(jax.ShapeDtypeStruct((M, 2, 4, CANDS),...]
    reshape x2 -> x0, local copies, waits for them, and re-layouts: 3.07 us -> none  [the longest x1 1.73 us: per_device(): return (coeffs.reshape(64, 4, CANDS), shapley.reshape(GROUPS, 4, CANDS))]
where the time goes in v3:
time: 251 us
  Pallas kernels  247 us (98%)
  local copies, waits for them, and re-layouts  3.07 us (1%)
    pallas_call x1, Pallas kernels, per_device(): pl.pallas_call(kernel, out_shape=(jax.ShapeDtypeStruct((M, 2, 4, CANDS),...  247 us

profile of v3, /device:TPU:11, one launch (start us, length us, event | category | flops | bytes accessed | tf_op | source)
XLA Modules:
  0.0 250.6 jit_solution(11266860247357116506)
XLA Ops:
  0.6 246.9 %shard_map.149 = (f32[32,2,4,256]{3,2,1,0:T(4,128)}, f32[10,4,256]{2,1,0:T(4,128)}) custom-call(bf16[4,4608]{1,0:T(4,128)(2,1)} %base_ref.1, bf16[10,4,4608]{2,1,0:T(4,128)(2,1)} %group_ref.1, f32[1,4608]{1,0:T(1,128)} %pre_ref.1, f32[1,4608]{1,0:T(1,128)} %post_ref.1, f32[4608]{0:T(1024)} %fin_gain_ref.1, f32[8,128]{1,0:T(8,128)} %constant.4.clone.cos_ref, ...), custom_call_target="tpu_custom_call" | custom-call | tf_op jit(solution)/shard_map/pallas_call | solution.py:637
  247.6 1.7 copy.18
  249.2 1.4 copy.19

commit v4 on v3

--- a/solution.py
+++ b/solution.py
@@ -538,12 +538,9 @@
 
         @pl.when(b == M - 1)
         def _():
-            read_end()
-
-        @pl.when(b == M)
-        def _():
             scatter(1, GROUP - END)
             exchange(send1, recv1, 1, 1)
+            read_end()
 
         @pl.when(b == M + 1)
         def _():

time: 251 us -> 248 us (0.988)
  Pallas kernels: 247 us -> 244 us
    pallas_call x1, Pallas kernels: 247 us -> 244 us  [per_device(): pl.pallas_call(kernel, out_shape=(jax.ShapeDtypeStruct((M, 2, 4, CANDS),...]
where the time goes in v4:
time: 248 us
  Pallas kernels  244 us (98%)
  local copies, waits for them, and re-layouts  3.07 us (1%)
    pallas_call x1, Pallas kernels, per_device(): pl.pallas_call(kernel, out_shape=(jax.ShapeDtypeStruct((M, 2, 4, CANDS),...  244 us

profile of v4, /device:TPU:11, one launch (start us, length us, event | category | flops | bytes accessed | tf_op | source)
XLA Modules:
  0.0 247.8 jit_solution(8018988216614340002)
XLA Ops:
  0.6 244.1 %shard_map.149 = (f32[32,2,4,256]{3,2,1,0:T(4,128)}, f32[10,4,256]{2,1,0:T(4,128)}) custom-call(bf16[4,4608]{1,0:T(4,128)(2,1)} %base_ref.1, bf16[10,4,4608]{2,1,0:T(4,128)(2,1)} %group_ref.1, f32[1,4608]{1,0:T(1,128)} %pre_ref.1, f32[1,4608]{1,0:T(1,128)} %post_ref.1, f32[4608]{0:T(1024)} %fin_gain_ref.1, f32[8,128]{1,0:T(8,128)} %constant.4.clone.cos_ref, ...), custom_call_target="tpu_custom_call" | custom-call | tf_op jit(solution)/shard_map/pallas_call | solution.py:634
  244.7 1.7 copy.18
  246.4 1.4 copy.19

commit v5 on v4

--- a/solution.py
+++ b/solution.py
@@ -173,7 +173,7 @@
     loads = [
         pltpu.make_async_copy(a, b, init_sem.at[i]) for i, (a, b) in enumerate(loads)
     ]
-    for load in loads:
+    for load in loads[:-1]:
         load.start()
 
     barrier = pltpu.get_barrier_semaphore()
@@ -206,6 +206,7 @@
 
     for load in loads[:-1]:
         load.wait()
+    loads[-1].start()
     kt[...] = key[...].T
 
     def turn_answers():

time: 248 us -> 248 us (level)
  no operation moved by 1% of the time
where the time goes in v5:
time: 248 us
  Pallas kernels  244 us (98%)
  local copies, waits for them, and re-layouts  3.07 us (1%)
    pallas_call x1, Pallas kernels, per_device(): pl.pallas_call(kernel, out_shape=(jax.ShapeDtypeStruct((M, 2, 4, CANDS),...  244 us

profile of v5, /device:TPU:11, one launch (start us, length us, event | category | flops | bytes accessed | tf_op | source)
XLA Modules:
  0.0 247.8 jit_solution(4224064683839572745)
XLA Ops:
  0.6 244.1 %shard_map.149 = (f32[32,2,4,256]{3,2,1,0:T(4,128)}, f32[10,4,256]{2,1,0:T(4,128)}) custom-call(bf16[4,4608]{1,0:T(4,128)(2,1)} %base_ref.1, bf16[10,4,4608]{2,1,0:T(4,128)(2,1)} %group_ref.1, f32[1,4608]{1,0:T(1,128)} %pre_ref.1, f32[1,4608]{1,0:T(1,128)} %post_ref.1, f32[4608]{0:T(1024)} %fin_gain_ref.1, f32[8,128]{1,0:T(8,128)} %constant.4.clone.cos_ref, ...), custom_call_target="tpu_custom_call" | custom-call | tf_op jit(solution)/shard_map/pallas_call | solution.py:635
  244.8 1.7 copy.18
  246.4 1.4 copy.19
